TPU v7x, 256 devices: a whole 4x4x8 slice. The times are simulated.
256 devices in a mesh: row: 32 (over z, y), col: 8 (over x, core).
Axes of the slice: x: 4, y: 4, z: 8, core: 2. Of those that a mesh axis runs over, the one named last changes fastest.
Arguments:
- tokens: bfloat16 [8192, 5376], P('row', 'col'), may hold values from -600 to 600, as said below
- input_gain: float32 [5376], P('col'), may hold values from 0.1 to 1.9
- q_gain: float32 [128], replicated, may hold values from 0.1 to 1.9
- k_gain: float32 [128], replicated, may hold values from 0.1 to 1.9
- wq: bfloat16 [5376, 2048], P('row', 'col'), may hold values from -0.078125 to 0.078125
- wk: bfloat16 [5376, 1024], P('row', 'col'), may hold values from -0.078125 to 0.078125
- wv: bfloat16 [5376, 1024], P('row', 'col'), may hold values from -0.078125 to 0.078125
- wo: bfloat16 [5376, 2048], P('row', 'col'), may hold values from -0.125 to 0.125
- upstream: bfloat16 [8192, 5376], P('row', 'col'), may hold values from -6 to 6
- doc_ids: int32 [8192], replicated, may hold values from 0 to 7, never falling along the last dimension, each value on 1 to 2048 neighbouring positions
- doc_labels: int32 [8], replicated, may hold values 0 or 1
Outputs:
- grad_input: bfloat16 [8192, 5376], P('row', 'col')
- grad_wq: bfloat16 [5376, 2048], P('row', 'col')
- grad_wk: bfloat16 [5376, 1024], P('row', 'col')
- grad_wv: bfloat16 [5376, 1024], P('row', 'col')
- grad_wo: bfloat16 [5376, 2048], P('row', 'col')
Inputs may be any that keep to these rules, and one draw needn't show every extreme that they name: Activations whose scales differ between tokens and between features. `doc_ids`: documents are numbered in order along the pack; each has 1 to 2048 tokens and one has exactly 2048.
All inputs are finite; a program needn't handle non-finite values.
Results may differ from a plain program's by a relative error of at most 0.02.
Values may be sent and summed in bfloat16 or wider, within the bound.
A program may use at most 64 MiB of HBM per device.

v0:
```python
import jax
import jax.numpy as jnp
from jax import lax
from jax.sharding import PartitionSpec as P

D = 5376
HQ = 16
HK = 8
HD = 128
WIN = 1024


epsilon = 1e-06
query_scale = 168.0 ** (-0.5)


def passed_along(block, axis, distance):
    devices = range(lax.axis_size(axis))
    route = [(i - distance, i) for i in devices if i - distance in devices]
    return lax.ppermute(block, axis, route)


def for_sending(array):

    def short(part):
        return part.astype(jnp.bfloat16) if part.dtype == jnp.float32 else part

    return jax.tree.map(short, array)


def rope_tables(positions):
    half_size = HD // 2
    frequency = 10000.0 ** (-(2.0 * jnp.arange(half_size, dtype=jnp.float32)) / HD)
    angles = positions[:, None] * frequency[None, :]
    return (jnp.cos(angles)[:, None, :], jnp.sin(angles)[:, None, :])


def rotate(values_in, cosine, sine):
    half_size = values_in.shape[-1] // 2
    first_half = values_in[..., :half_size]
    second_half = values_in[..., half_size:]
    return jnp.concatenate(
        [first_half * cosine - second_half * sine, second_half * cosine + first_half * sine], -1
    )


def rotate_back(grads_in, cosine, sine):
    half_size = grads_in.shape[-1] // 2
    first_half = grads_in[..., :half_size]
    second_half = grads_in[..., half_size:]
    return jnp.concatenate(
        [first_half * cosine + second_half * sine, second_half * cosine - first_half * sine], -1
    )


def head_norm(values_in):
    scaling = lax.rsqrt(jnp.mean(values_in * values_in, -1, keepdims=True) + epsilon)
    return (values_in * scaling, scaling)


def head_norm_back(grad_unit, unit_values, scaling):
    return scaling * (
        grad_unit - unit_values * jnp.mean(grad_unit * unit_values, -1, keepdims=True)
    )


def attend(queries, keys_in, values_in, d_attn, allowed):
    f32 = jnp.float32
    scores = jnp.einsum("tkgd,skd->kgts", queries, keys_in, preferred_element_type=f32)
    weights = jnp.where(allowed[None, None], jnp.exp(scores), 0.0)
    probs = weights / jnp.sum(weights, -1, keepdims=True)
    probs_low = probs.astype(jnp.bfloat16)
    attended = jnp.einsum(
        "kgts,skd->tkgd", probs_low, values_in, preferred_element_type=f32
    ).astype(jnp.bfloat16)
    d_prob = jnp.einsum("tkgd,skd->kgts", d_attn, values_in, preferred_element_type=f32)
    delta = jnp.sum(probs * d_prob, -1, keepdims=True)
    d_score = (probs * (d_prob - delta)).astype(jnp.bfloat16)
    d_query = jnp.einsum("kgts,skd->tkgd", d_score, keys_in, preferred_element_type=f32)
    d_key = jnp.einsum("kgts,tkgd->skd", d_score, queries, preferred_element_type=f32)
    d_value = jnp.einsum("kgts,tkgd->skd", probs_low, d_attn, preferred_element_type=f32)
    return (attended, d_query, d_key, d_value)


def contract_last(left_rows, right_rows):
    return lax.dot_general(
        left_rows, right_rows, (((1,), (1,)), ((), ())), preferred_element_type=jnp.float32
    )


def contract_first(left_rows, right_rows):
    return lax.dot_general(
        left_rows, right_rows, (((0,), (0,)), ((), ())), preferred_element_type=jnp.float32
    )


def per_device(tokens, input_gain, q_gain, k_gain, wq, wk, wv, wo, upstream, doc_ids, doc_labels):
    f32 = jnp.float32
    bf16 = jnp.bfloat16
    tok_rows = tokens.shape[0]
    first_token = lax.axis_index("row") * tok_rows
    features = tokens.astype(f32)
    total_sq = lax.psum(jnp.sum(features * features, 1), "col")
    scale_in = lax.rsqrt(total_sq[:, None] / D + epsilon)
    unit_in = features * scale_in
    normed = (unit_in * input_gain).astype(bf16)
    doc_queries = lax.dynamic_slice_in_dim(doc_ids, first_token, tok_rows, 0)
    member = (
        doc_queries[:, None] == jnp.arange(doc_labels.shape[0], dtype=jnp.int32)[None, :]
    ).astype(jnp.int32)
    forget = jnp.sum(member * doc_labels[None, :], 1)
    token_sign = (1 - 2 * forget).astype(f32)
    cotangent = (token_sign[:, None] * upstream.astype(f32)).astype(bf16)
    normed_all, cotangent_all = (
        lax.all_gather(normed, "col", axis=1, tiled=True),
        lax.all_gather(cotangent, "col", axis=1, tiled=True),
    )
    q_width = wq.shape[1]
    k_width = wk.shape[1]
    w_stack = jnp.concatenate([wq, wk, wv], 1)
    columns = normed_all
    projected = jnp.dot(
        columns, lax.all_gather(w_stack, "row", axis=0, tiled=True), preferred_element_type=f32
    )
    q_heads = q_width // HD
    k_heads = k_width // HD
    group_size = HQ // HK
    q_proj = projected[:, :q_width].reshape(tok_rows, q_heads, HD)
    k_proj = projected[:, q_width : q_width + k_width].reshape(tok_rows, k_heads, HD)
    values = projected[:, q_width + k_width :].astype(bf16)
    positions = (first_token + jnp.arange(tok_rows, dtype=jnp.int32)).astype(f32)
    cosine, sine = rope_tables(positions)
    unit_q, scale_q = head_norm(q_proj)
    query = (rotate(unit_q * q_gain, cosine, sine) * query_scale).astype(bf16)
    unit_k, scale_k = head_norm(k_proj)
    key = rotate(unit_k * k_gain, cosine, sine).astype(bf16)
    local_kv = jnp.stack([key.reshape(tok_rows, k_width), values])
    depth = -(-WIN // tok_rows)
    earlier = []
    moving = local_kv
    for hop_index in range(depth):
        moving = passed_along(moving, "row", 1)
        earlier.insert(0, moving)
    all_kv = jnp.concatenate(earlier + [local_kv], 1)
    key_span = (depth + 1) * tok_rows
    key_pos = first_token - depth * tok_rows + jnp.arange(key_span, dtype=jnp.int32)
    doc_keys = jnp.take(doc_ids, jnp.clip(key_pos, 0, doc_ids.shape[0] - 1))
    query_pos = first_token + jnp.arange(tok_rows, dtype=jnp.int32)
    offsets = query_pos[:, None] - key_pos[None, :]
    allowed = (
        (offsets >= 0)
        & (offsets < WIN)
        & (key_pos[None, :] >= 0)
        & (doc_queries[:, None] == doc_keys[None, :])
    )
    columns = cotangent_all
    d_attn = jnp.dot(
        columns, lax.all_gather(wo, "row", axis=0, tiled=True), preferred_element_type=f32
    ).astype(bf16)
    attended, d_query, d_key, d_value = attend(
        query.reshape(tok_rows, k_heads, group_size, HD),
        all_kv[0].reshape(key_span, k_heads, HD),
        all_kv[1].reshape(key_span, k_heads, HD),
        d_attn.reshape(tok_rows, k_heads, group_size, HD),
        allowed,
    )
    attn = attended.reshape(tok_rows, q_width)
    grad_kv = jnp.stack([d_key.reshape(key_span, k_width), d_value.reshape(key_span, k_width)])
    earlier_grads = [
        grad_kv[:, block_index * tok_rows : (block_index + 1) * tok_rows]
        for block_index in range(depth)
    ]
    own_grads = grad_kv[:, depth * tok_rows :]
    carried = jnp.zeros_like(own_grads)
    for block_index in range(depth):
        carried = passed_along(for_sending(carried + earlier_grads[block_index]), "row", -1)
    own_grads = own_grads + carried
    grad_q_act = head_norm_back(
        rotate_back(d_query.reshape(tok_rows, q_heads, HD), cosine, sine) * query_scale * q_gain,
        unit_q,
        scale_q,
    )
    grad_q_act = grad_q_act.astype(bf16).reshape(tok_rows, q_width)
    grad_k_act = head_norm_back(
        rotate_back(own_grads[0].reshape(tok_rows, k_heads, HD), cosine, sine) * k_gain,
        unit_k,
        scale_k,
    )
    grad_k_act = grad_k_act.astype(bf16).reshape(tok_rows, k_width)
    grad_v_act = own_grads[1].astype(bf16)
    grad_stack = jnp.concatenate([grad_q_act, grad_k_act, grad_v_act], 1)
    head_terms = contract_last(grad_stack, lax.all_gather(w_stack, "row", axis=0, tiled=True))
    d_normed = lax.psum_scatter(
        head_terms.astype(jnp.bfloat16), "col", scatter_dimension=1, tiled=True
    ).astype(jnp.float32)
    scaled_grad = d_normed * input_gain
    inner_sum = lax.psum(jnp.sum(scaled_grad * unit_in, 1), "col")
    grad_input = (scale_in * (scaled_grad - unit_in * inner_sum[:, None] / D)).astype(bf16)
    projection_part = contract_first(normed_all, grad_stack)
    output_part = contract_first(cotangent_all, attn)
    weight_sums = lax.psum_scatter(
        jnp.concatenate([projection_part, output_part], 1).astype(jnp.bfloat16),
        "row",
        scatter_dimension=0,
        tiled=True,
    ).astype(jnp.float32)
    grad_wq = weight_sums[:, :q_width].astype(bf16)
    grad_wk = weight_sums[:, q_width : q_width + k_width].astype(bf16)
    grad_wv = weight_sums[:, q_width + k_width : q_width + 2 * k_width].astype(bf16)
    grad_wo = weight_sums[:, q_width + 2 * k_width :].astype(bf16)
    return (grad_input, grad_wq, grad_wk, grad_wv, grad_wo)


def solution(mesh):
    in_specs = (
        P("row", "col"),
        P("col"),
        P(),
        P(),
        P("row", "col"),
        P("row", "col"),
        P("row", "col"),
        P("row", "col"),
        P("row", "col"),
        P(),
        P(),
    )
    out_specs = (
        P("row", "col"),
        P("row", "col"),
        P("row", "col"),
        P("row", "col"),
        P("row", "col"),
    )
    return jax.shard_map(
        per_device, mesh=mesh, in_specs=in_specs, out_specs=out_specs, check_vma=False
    )
```

profile of v0, /device:TPU:1, one launch (start us, length us, event | category | flops | bytes accessed | tf_op | source)
XLA Modules:
  0.0 604.0 jit_solution(572762923404852251)
XLA Ops:
  8.7 1.8 multiply_convert_fusion.1
  12.4 15.0 %psum.14 = f32[256]{0:T(256)S(1)} all-reduce(f32[256]{0:T(256)S(1)} %fusion.21), channel_id=1, replica_groups=mesh['row'=32,'col'=8] {'col'}, use_global_device_ids=true, to_apply=%region_1.0 | all-reduce | flops 256 | bytes 2048 | tf_op jit(solution)/shard_map/psum | solution.py:103
  27.5 1.9 fusion.15
  29.4 1.6 pad_maximum_fusion.4
  31.2 7.1 %gather_fusion = s32[1280]{0:T(1024)S(1)} fusion(s32[8192]{0:T(1024)S(1)} %copy-done, s32[2048]{0:T(1024)S(1)} %pad_clamp_fusion), kind=kCustom, calls=%fused_computation | custom fusion | bytes 15360 | tf_op jit(solution)/shard_map/jit(_take)/gather | solution.py:147
  40.0 3.8 all-gather.9.cloned.1.call-done
  43.8 78.5 %all-gather.11.cloned.1.call-done = bf16[5376,256]{1,0:T(8,128)(2,1)} async-done(((bf16[168,256]{1,0:T(8,128)(2,1)}), bf16[5376,256]{1,0:T(8,128)(2,1)}) %all-gather.11.cloned.1.call-update) | async-done | bytes 2752528 | tf_op jit(solution)/shard_map/all_gather | solution.py:158
  122.3 3.8 convolution_convert_fusion.3
  126.1 28.4 %all-gather.5.cloned.1.call-done = bf16[256,5376]{0,1:T(8,128)(2,1)} async-done(((bf16[256,672]{0,1:T(8,128)(2,1)}), bf16[256,5376]{0,1:T(8,128)(2,1)}) %all-gather.5.cloned.1.call-update) | async-done | bytes 2752528 | tf_op jit(solution)/shard_map/all_gather | solution.py:115
  154.6 86.7 %all-gather.7.cloned.1.call-done = bf16[5376,512]{1,0:T(8,128)(2,1)} async-done(((bf16[168,512]{1,0:T(8,128)(2,1)}), bf16[5376,512]{1,0:T(8,128)(2,1)}) %all-gather.7.cloned.1.call-update) | async-done | bytes 5505040 | tf_op jit(solution)/shard_map/all_gather | solution.py:123
  241.3 5.0 fusion.71
  247.5 1.9 collective-permute-start
  251.2 3.8 collective-permute-start.1
  255.0 1.9 collective-permute-done.1
  256.9 3.8 collective-permute-start.2
  260.9 1.8 collective-permute-done.2
  262.6 3.8 collective-permute-start.3
  266.9 2.3 collective-permute-done.3
  274.7 4.7 collective-permute-done.4
  281.1 6.9 %collective-permute-done.5 = bf16[2,256,128]{2,1,0:T(8,128)(2,1)S(1)} collective-permute-done((bf16[2,256,128]{2,1,0:T(8,128)(2,1)S(1)}, bf16[2,256,128]{2,1,0:T(8,128)(2,1)S(1)}, u32[]{:S(2)}, u32[]{:S(2)}) %collective-permute-start.5) | collective-permute-done | bytes 131104 | tf_op jit(solution)/shard_map/ppermute | solution.py:20
  289.5 7.5 %collective-permute-done.6 = bf16[2,256,128]{2,1,0:T(8,128)(2,1)S(1)} collective-permute-done((bf16[2,256,128]{2,1,0:T(8,128)(2,1)S(1)}, bf16[2,256,128]{2,1,0:T(8,128)(2,1)S(1)}, u32[]{:S(2)}, u32[]{:S(2)}) %collective-permute-start.6) | collective-permute-done | bytes 131104 | tf_op jit(solution)/shard_map/ppermute | solution.py:20
  299.3 6.8 %collective-permute-done.7 = bf16[2,256,128]{2,1,0:T(8,128)(2,1)S(1)} collective-permute-done((bf16[2,256,128]{2,1,0:T(8,128)(2,1)S(1)}, bf16[2,256,128]{2,1,0:T(8,128)(2,1)S(1)}, u32[]{:S(2)}, u32[]{:S(2)}) %collective-permute-start.7) | collective-permute-done | bytes 131104 | tf_op jit(solution)/shard_map/ppermute | solution.py:20
  307.2 5.7 convolution_convert_fusion.2
  313.0 1.7 copy-done.5
  318.3 4.1 convolution_convert_fusion
  322.4 6.3 %pad_maximum_fusion = bf16[5376,768]{0,1:T(8,128)(2,1)} fusion(bf16[5376,256]{0,1:T(8,128)(2,1)S(1)} %convolution_convert_fusion.1, bf16[5376,512]{0,1:T(8,128)(2,1)} %convolution_convert_fusion), kind=kLoop, calls=%fused_computation.2 | loop fusion | flops 16515072 | bytes 16515072 | tf_op jit(solution)/shard_map/concatenate | solution.py:202
  328.7 11.8 %copy.150 = bf16[5376,768]{1,0:T(8,128)(2,1)} copy(bf16[5376,768]{0,1:T(8,128)(2,1)} %pad_maximum_fusion) | data formatting | bytes 16515072
  340.5 31.0 %reduce-scatter.5.cloned.1.call-done = bf16[256,672]{0,1:T(8,128)(2,1)} async-done(((bf16[256,5376]{0,1:T(8,128)(2,1)}), bf16[256,672]{0,1:T(8,128)(2,1)}) %reduce-scatter.5.cloned.1.call-update) | async-done | bytes 344080 | tf_op jit(solution)/shard_map/reduce_scatter | solution.py:193
  372.7 15.1 %psum.15 = f32[256]{0:T(256)S(1)} all-reduce(f32[256]{0:T(256)S(1)} %fusion.16), channel_id=1, replica_groups=mesh['row'=32,'col'=8] {'col'}, use_global_device_ids=true, to_apply=%region_11.12 | all-reduce | flops 256 | bytes 2048 | tf_op jit(solution)/shard_map/psum | solution.py:197
  387.8 1.9 fusion.20
  389.7 204.4 %reduce-scatter.7.cloned.1.call-done = bf16[168,768]{1,0:T(8,128)(2,1)} async-done(((bf16[5376,768]{1,0:T(8,128)(2,1)}), bf16[168,768]{1,0:T(8,128)(2,1)}) %reduce-scatter.7.cloned.1.call-update) | async-done | bytes 258064
  594.1 1.6 fusion.68
  (100 shorter events, 26.9 us)
Async XLA Ops:
  7.2 24.0 %copy-start = (s32[8192]{0:T(1024)S(1)}, s32[8192]{0:T(1024)}, u32[]{:S(2)}) copy-start(s32[8192]{0:T(1024)} %param.20) | copy-start | bytes 98308
  7.2 36.6 %all-gather.9.cloned.1.call-start = ((), (), s32[]{:S(2)}) async-start(), calls=%async_computation.4 | async-start | bytes 3096576 | tf_op jit(solution)/shard_map/all_gather | solution.py:116
  10.5 111.8 %all-gather.11.cloned.1.call-start = ((), (), s32[]{:S(2)}) async-start(), calls=%async_computation.5 | async-start | bytes 2838528 | tf_op jit(solution)/shard_map/all_gather | solution.py:158
  11.3 143.3 %all-gather.5.cloned.1.call-start = ((), (), s32[]{:S(2)}) async-start(), calls=%async_computation.2 | async-start | bytes 3096576 | tf_op jit(solution)/shard_map/all_gather | solution.py:115
  29.4 211.9 %all-gather.7.cloned.1.call-start = ((), (), s32[]{:S(2)}) async-start(), calls=%async_computation.3 | async-start | bytes 5677056 | tf_op jit(solution)/shard_map/all_gather | solution.py:123
  31.1 340.5 %reduce-scatter.5.cloned.1.call-start = ((), (), s32[]{:S(2)}) async-start(), calls=%async_computation.6 | async-start | bytes 3096576 | tf_op jit(solution)/shard_map/reduce_scatter | solution.py:193
  31.2 7.2 %copy-start.9 = (f32[128]{0:T(128)S(1)}, f32[128]{0:T(128)}, u32[]{:S(2)}) copy-start(f32[128]{0:T(128)} %param.13) | copy-start | bytes 1540
  126.1 120.5 %copy-start.8 = (f32[128]{0:T(128)S(1)}, f32[128]{0:T(128)}, u32[]{:S(2)}) copy-start(f32[128]{0:T(128)} %param.14) | copy-start | bytes 1540
  247.5 3.8 collective-permute-start
  251.2 5.7 collective-permute-start.1
  256.9 5.7 collective-permute-start.2
  262.6 6.6 %collective-permute-start.3 = (bf16[2,256,128]{2,1,0:T(8,128)(2,1)S(1)}, bf16[2,256,128]{2,1,0:T(8,128)(2,1)S(1)}, u32[]{:S(2)}, u32[]{:S(2)}) collective-permute-start(bf16[2,256,128]{2,1,0:T(8,128)(2,1)S(1)} %collective-permute-done.2), channel_id=1, source_target_pairs={{0,8},{8,16},{16,24},{24,32},{32,40},{40,48},{48,56},{56,64},{64,7... | collective-permute-start | bytes 393224 | tf_op jit(solution)/shard_map/ppermute | solution.py:20
  269.4 3.1 copy-start.6
  270.1 1.6 copy-start.4
  273.2 6.2 %collective-permute-start.4 = (bf16[2,256,128]{2,1,0:T(8,128)(2,1)S(1)}, bf16[2,256,128]{2,1,0:T(8,128)(2,1)S(1)}, u32[]{:S(2)}, u32[]{:S(2)}) collective-permute-start(bf16[2,256,128]{2,1,0:T(8,128)(2,1)S(1)} %fusion.30), channel_id=1, source_target_pairs={{8,0},{16,8},{24,16},{32,24},{40,32},{48,40},{56,48},{64,56},{72,6... | collective-permute-start | bytes 393224 | tf_op jit(solution)/shard_map/ppermute | solution.py:20
  279.4 8.6 %collective-permute-start.5 = (bf16[2,256,128]{2,1,0:T(8,128)(2,1)S(1)}, bf16[2,256,128]{2,1,0:T(8,128)(2,1)S(1)}, u32[]{:S(2)}, u32[]{:S(2)}) collective-permute-start(bf16[2,256,128]{2,1,0:T(8,128)(2,1)S(1)} %fusion.33), channel_id=1, source_target_pairs={{8,0},{16,8},{24,16},{32,24},{40,32},{48,40},{56,48},{64,56},{72,6... | collective-permute-start | bytes 393224 | tf_op jit(solution)/shard_map/ppermute | solution.py:20
  288.0 9.0 %collective-permute-start.6 = (bf16[2,256,128]{2,1,0:T(8,128)(2,1)S(1)}, bf16[2,256,128]{2,1,0:T(8,128)(2,1)S(1)}, u32[]{:S(2)}, u32[]{:S(2)}) collective-permute-start(bf16[2,256,128]{2,1,0:T(8,128)(2,1)S(1)} %fusion.26), channel_id=1, source_target_pairs={{8,0},{16,8},{24,16},{32,24},{40,32},{48,40},{56,48},{64,56},{72,6... | collective-permute-start | bytes 393224 | tf_op jit(solution)/shard_map/ppermute | solution.py:20
  297.0 9.1 %collective-permute-start.7 = (bf16[2,256,128]{2,1,0:T(8,128)(2,1)S(1)}, bf16[2,256,128]{2,1,0:T(8,128)(2,1)S(1)}, u32[]{:S(2)}, u32[]{:S(2)}) collective-permute-start(bf16[2,256,128]{2,1,0:T(8,128)(2,1)S(1)} %fusion.38), channel_id=1, source_target_pairs={{8,0},{16,8},{24,16},{32,24},{40,32},{48,40},{56,48},{64,56},{72,6... | collective-permute-start | bytes 393224 | tf_op jit(solution)/shard_map/ppermute | solution.py:20
  312.9 1.7 copy-start.5
  313.0 281.1 %reduce-scatter.7.cloned.1.call-start = ((), (), s32[]{:S(2)}) async-start(), calls=%async_computation.7 | async-start | bytes 8515584
  314.7 1.9 copy-start.2
  316.5 1.8 copy-start.1
  340.5 31.1 %copy-start.3 = (bf16[256,672]{0,1:T(8,128)(2,1)S(1)}, bf16[256,672]{0,1:T(8,128)(2,1)}, u32[]{:S(2)}) copy-start(bf16[256,672]{0,1:T(8,128)(2,1)} %param.11) | copy-start | bytes 1032196
  340.5 31.1 %copy-start.7 = (f32[672]{0:T(1024)S(1)}, f32[672]{0:T(1024)}, u32[]{:S(2)}) copy-start(f32[672]{0:T(1024)} %param.12) | copy-start | bytes 8068
Sparse Core Ops, SparseCore 0:
  10.7 33.1 all-gather.8
  46.4 75.8 all-gather.10
  124.7 29.8 all-gather.4
  157.0 84.2 all-gather.6
  313.1 58.4 reduce-scatter.4
  376.0 218.0 reduce-scatter.6
where the time goes:
time: 608 us; the launch traced here: 604 us
  waiting for transfers between devices  467 us (77%)
  blocking collectives  30.1 us (5%)
  local copies, waits for them, and re-layouts  27.5 us (5%)
  matrix products  23.7 us (4%)
  other arithmetic  22.1 us (4%)
  starting transfers between devices  18.8 us (3%)
  between operations  14.6 us (2%)
    unnamed x7, waiting for transfers between devices  205 us
    all_gather x1, waiting for transfers between devices, per_device(): lax.all_gather(w_stack, 'row', axis=0, tiled=True)  86.7 us
    all_gather x1, waiting for transfers between devices, per_device(): lax.all_gather(wo, 'row', axis=0, tiled=True)  78.5 us
    ppermute x8, waiting for transfers between devices, passed_along(): return lax.ppermute(block, axis, route)  33.6 us
    reduce_scatter x1, waiting for transfers between devices, per_device(): lax.psum_scatter(head_terms.astype(jnp.bfloat16), 'col', scatter_dimensio...  31 us
    all_gather x1, waiting for transfers between devices, per_device(): lax.all_gather(normed, 'col', axis=1, tiled=True)  28.4 us
    ppermute x8, starting transfers between devices, passed_along(): return lax.ppermute(block, axis, route)  18.5 us
    unnamed x26, local copies, waits for them, and re-layouts  15.5 us
  transfers between devices with their start and end apart: 14, of which 14 were waited for; matrix products, arithmetic and copies ran while one was open for 8% of the time, Pallas kernels for 0%

commit v1 on v0

v1 whole, which is shorter than its diff:
```python
import jax
import jax.numpy as jnp
from jax import lax
from jax.sharding import Mesh
from jax.sharding import PartitionSpec as P

D = 5376
HD = 128
WIN = 1024
epsilon = 1e-06
query_scale = 168.0 ** (-0.5)
f32 = jnp.float32
bf16 = jnp.bfloat16


def tables(row, tok):
    half = HD // 2
    positions = (row * tok + jnp.arange(tok, dtype=jnp.int32)).astype(f32)
    frequency = 10000.0 ** (-(2.0 * jnp.arange(half, dtype=f32)) / HD)
    angles = frequency[:, None] * positions[None, :]
    return jnp.cos(angles), jnp.sin(angles)


def rot(v, c, s):
    a, b = v[: HD // 2], v[HD // 2 :]
    return jnp.concatenate([a * c - b * s, b * c + a * s], 0)


def unit(p):
    sc = lax.rsqrt(jnp.mean(p * p, 0, keepdims=True) + epsilon)
    return p * sc, sc


def unit_back(w, u, sc):
    return sc * (w - u * jnp.mean(w * u, 0, keepdims=True))


def per_device(tokens, input_gain, q_gain, k_gain, wq, wk, wv, wo, upstream, doc_ids, doc_labels):
    tok = tokens.shape[0]
    nz, ny = lax.axis_size("z"), lax.axis_size("y")
    nrow = nz * ny
    row = lax.axis_index("z") * ny + lax.axis_index("y")
    col = ("x", "k")
    fr = wq.shape[0]
    x32 = tokens.astype(f32)
    ss = lax.psum(jnp.sum(x32 * x32, 1), col)
    scale = lax.rsqrt(ss / D + epsilon)[None, :]
    docs = lax.dynamic_slice_in_dim(doc_ids, row * tok, tok, 0)
    member = (docs[:, None] == jnp.arange(doc_labels.shape[0], dtype=jnp.int32)[None, :]).astype(jnp.int32)
    sign = (1 - 2 * jnp.sum(member * doc_labels[None, :], 1)).astype(f32)
    before = jnp.sum((doc_ids[None, :] < jnp.arange(doc_labels.shape[0])[:, None]).astype(jnp.int32), 1)
    start = jnp.sum(member * before[None, :], 1)
    pos = row * tok + jnp.arange(tok, dtype=jnp.int32)
    low = jnp.maximum(start, pos - (WIN - 1))
    xg = (x32 * input_gain).astype(bf16).T.reshape(ny, fr, tok)
    ct = (upstream.astype(f32) * sign[:, None]).astype(bf16).T.reshape(ny, fr, tok)
    xa = lax.all_to_all(xg, "y", 0, 0)
    ca = lax.all_to_all(ct, "y", 0, 0)
    X = lax.all_gather(xa, col)
    C = lax.all_gather(ca, col)
    W = lax.all_gather(jnp.concatenate([wq, wk, wv, wo], 1), "z")
    qkv = jnp.einsum("cfh,cyft->yht", W[:, :, :512], X, preferred_element_type=f32).astype(bf16)
    dat = jnp.einsum("cfh,cyft->yht", W[:, :, 512:], C, preferred_element_type=f32).astype(bf16)
    proj = lax.psum_scatter(qkv, "y", scatter_dimension=0).astype(f32) * scale
    dA = lax.psum_scatter(dat, "y", scatter_dimension=0).astype(bf16)
    c, s = tables(row, tok)
    qgc, kgc = q_gain[:, None], k_gain[:, None]
    uq0, sq0 = unit(proj[:128])
    uq1, sq1 = unit(proj[128:256])
    uk, sk = unit(proj[256:384])
    vT = proj[384:].astype(bf16)
    q = jnp.concatenate([rot(uq0 * qgc, c, s), rot(uq1 * qgc, c, s)], 1) * query_scale
    q = q.astype(bf16)
    da = jnp.concatenate([dA[:128], dA[128:]], 1)
    kT = rot(uk * kgc, c, s).astype(bf16)
    kv = jnp.stack([kT, vT])
    blocks = [kv]
    for d in range(1, 5):
        route = [(i, (i + d) % nrow) for i in range(nrow)]
        blocks.append(lax.ppermute(kv, ("z", "y"), route))
    low2 = jnp.concatenate([low, low])[None, :]
    pos2 = jnp.concatenate([pos, pos])[None, :]
    es = []
    total = 0.0
    for d in range(5):
        sp = ((row - d) * tok + jnp.arange(tok, dtype=jnp.int32))[:, None]
        ok = (sp >= low2) & (sp <= pos2)
        sc = jnp.einsum("ds,dt->st", blocks[d][0], q, preferred_element_type=f32)
        e = jnp.where(ok, jnp.exp(sc), 0.0)
        es.append(e)
        total = total + jnp.sum(e, 0, keepdims=True)
    inv = 1.0 / total
    attn = 0.0
    for d in range(5):
        attn = attn + jnp.einsum("ds,st->dt", blocks[d][1], (es[d] * inv).astype(bf16), preferred_element_type=f32)
    delta = jnp.sum(attn * da.astype(f32), 0, keepdims=True)
    dq = 0.0
    dkv = 0.0
    for d in range(5):
        p = es[d] * inv
        dp = jnp.einsum("ds,dt->st", blocks[d][1], da, preferred_element_type=f32)
        ds = (p * (dp - delta)).astype(bf16)
        dq = dq + jnp.einsum("ds,st->dt", blocks[d][0], ds, preferred_element_type=f32)
        dk = jnp.einsum("dt,st->ds", q, ds, preferred_element_type=f32)
        dv = jnp.einsum("dt,st->ds", da, p.astype(bf16), preferred_element_type=f32)
        part = jnp.stack([dk, dv])
        if d:
            route = [(i, (i - d) % nrow) for i in range(nrow)]
            part = lax.ppermute(part.astype(bf16), ("z", "y"), route).astype(f32)
        dkv = dkv + part
    g0 = unit_back(rot(dq[:, :tok], c, -s) * query_scale * qgc, uq0, sq0)
    g1 = unit_back(rot(dq[:, tok:], c, -s) * query_scale * qgc, uq1, sq1)
    gk = unit_back(rot(dkv[0], c, -s) * kgc, uk, sk)
    G = jnp.concatenate([g0, g1, gk, dkv[1]], 0) * scale
    inner = lax.psum(jnp.sum(G * proj, 0), col) / D
    at = jnp.concatenate([attn[:, :tok], attn[:, tok:]], 0).astype(bf16)
    GA = lax.all_gather(jnp.concatenate([G.astype(bf16), at], 0), "y")
    dn = jnp.einsum("cfh,yht->cyft", W[:, :, :512], GA[:, :512], preferred_element_type=f32).astype(bf16)
    dn = lax.psum_scatter(dn.reshape(8, ny, fr, tok), col, scatter_dimension=0)
    dn = lax.all_to_all(dn, "y", 0, 0).reshape(ny * fr, tok).astype(f32).T
    grad_input = (dn * input_gain - x32 * scale[0][:, None] * inner[:, None]).astype(bf16)
    dw = jnp.einsum("cyft,yht->cfh", X, GA[:, :512], preferred_element_type=f32)
    dwo = jnp.einsum("cyft,yht->cfh", C, GA[:, 512:], preferred_element_type=f32)
    dw = lax.psum_scatter(jnp.concatenate([dw, dwo], 2).astype(bf16), "z", scatter_dimension=0)
    return grad_input, dw[:, :256], dw[:, 256:384], dw[:, 384:512], dw[:, 512:]


def solution(mesh):
    fine = Mesh(mesh.devices.reshape(8, 4, 4, 2), ("z", "y", "x", "k"))
    rc = P(("z", "y"), ("x", "k"))
    return jax.shard_map(
        per_device,
        mesh=fine,
        in_specs=(rc, P(("x", "k")), P(), P(), rc, rc, rc, rc, rc, P(), P()),
        out_specs=(rc,) * 5,
        check_vma=False,
    )
```

time: 608 us -> 369 us (0.61)
  waiting for transfers between devices: 467 us -> 243 us
  local copies, waits for them, and re-layouts: 27.5 us -> 10.1 us
  blocking collectives: 30.1 us -> 46.6 us
  other arithmetic: 22.1 us -> 12 us
    unnamed x7 -> x9, waiting for transfers between devices: 205 us -> 64 us
    all_gather x4, waiting for transfers between devices: 197 us -> 112 us  [the longest x1 33.5 us: per_device(): C = lax.all_gather(ca, col)]
    reduce_scatter x1 -> x3, waiting for transfers between devices: 31 us -> 55.8 us  [the longest x1 27.6 us: per_device(): proj = lax.psum_scatter(qkv, 'y', scatter_dimension=0).astype(f32) * scale]
    ppermute x8, waiting for transfers between devices: 33.6 us -> 11.2 us  [the longest x4 8.48 us: per_device(): blocks.append(lax.ppermute(kv, ('z', 'y'), route))]
    all_to_all x0 -> x2, blocking collectives: none -> 20 us  [the longest x1 10.9 us: per_device(): ca = lax.all_to_all(ct, 'y', 0, 0)]
    unnamed x26 -> x17, local copies, waits for them, and re-layouts: 15.5 us -> 1.26 us
    ppermute x8, starting transfers between devices: 18.5 us -> 9.61 us  [the longest x4 5.22 us: per_device(): part = lax.ppermute(part.astype(bf16), ('z', 'y'), route).astype(f32)]
    gather x1 -> x0, local copies, waits for them, and re-layouts: 7.08 us -> none  [per_device(): doc_keys = jnp.take(doc_ids, jnp.clip(key_pos, 0, doc_ids.shape[0] - 1))]
  transfers between devices with their start and end apart: 14 -> 17, of which waited for: 14 -> 14; matrix products, arithmetic and copies ran while one was open for 8% -> 8% of each run, Pallas kernels for 0% -> 0%
where the time goes in v1:
time: 369 us; the launch traced here: 366 us
  waiting for transfers between devices  243 us (66%)
  blocking collectives  46.6 us (13%)
  matrix products  25.4 us (7%)
  between operations  14.7 us (4%)
  starting transfers between devices  13.9 us (4%)
  other arithmetic  12 us (3%)
  local copies, waits for them, and re-layouts  10.1 us (3%)
    unnamed x9, waiting for transfers between devices  64 us
    all_gather x1, waiting for transfers between devices, per_device(): C = lax.all_gather(ca, col)  33.5 us
    all_gather x1, waiting for transfers between devices, per_device(): GA = lax.all_gather(jnp.concatenate([G.astype(bf16), at], 0), 'y')  32.4 us
    reduce_scatter x1, waiting for transfers between devices, per_device(): proj = lax.psum_scatter(qkv, 'y', scatter_dimension=0).astype(f32) * scale  27.6 us
    all_gather x1, waiting for transfers between devices, per_device(): X = lax.all_gather(xa, col)  27.3 us
    reduce_scatter x1, waiting for transfers between devices, per_device(): lax.psum_scatter(jnp.concatenate([dw, dwo], 2).astype(bf16), 'z', scatter...  20.3 us
    all_gather x1, waiting for transfers between devices, per_device(): W = lax.all_gather(jnp.concatenate([wq, wk, wv, wo], 1), 'z')  18.7 us
    psum x1, blocking collectives, per_device(): inner = lax.psum(jnp.sum(G * proj, 0), col) / D  14.6 us
  transfers between devices with their start and end apart: 17, of which 14 were waited for; matrix products, arithmetic and copies ran while one was open for 8% of the time, Pallas kernels for 0%

profile of v1, /device:TPU:1, one launch (start us, length us, event | category | flops | bytes accessed | tf_op | source)
XLA Modules:
  0.0 365.6 jit_solution(6928386804928171330)
XLA Ops:
  7.2 1.7 pad_maximum_fusion.2
  12.5 10.9 %all_to_all.15 = bf16[4,168,256]{2,1,0:T(8,128)(2,1)} all-to-all(bf16[4,168,256]{2,1,0:T(8,128)(2,1)S(1)} %bitcast.188), channel_id=1, replica_groups=mesh['z'=8,'y'=4,'x'=4,'k'=2] {'y'}, dimensions={0} | all-to-all | bytes 688128 | tf_op jit(solution)/shard_map/all_to_all | solution.py:58
  23.7 9.0 %all_to_all.16 = bf16[4,168,256]{2,1,0:T(8,128)(2,1)} all-to-all(bf16[4,168,256]{2,1,0:T(8,128)(2,1)S(1)} %bitcast.187), channel_id=1, replica_groups=mesh['z'=8,'y'=4,'x'=4,'k'=2] {'y'}, dimensions={0} | all-to-all | bytes 688128 | tf_op jit(solution)/shard_map/all_to_all | solution.py:57
  32.8 18.7 %all-gather.11.cloned.1.call-done = bf16[1344,768]{1,0:T(8,128)(2,1)} async-done(((bf16[168,768]{1,0:T(8,128)(2,1)}), bf16[1344,768]{1,0:T(8,128)(2,1)}) %all-gather.11.cloned.1.call-update) | async-done | bytes 2064400 | tf_op jit(solution)/shard_map/all_gather | solution.py:61
  51.5 33.5 %all-gather.13.cloned.1.call-done = bf16[32,168,256]{2,1,0:T(8,128)(2,1)} async-done(((bf16[4,168,256]{2,1,0:T(8,128)(2,1)}), bf16[32,168,256]{2,1,0:T(8,128)(2,1)}) %all-gather.13.cloned.1.call-update) | async-done | bytes 2752528 | tf_op jit(solution)/shard_map/all_gather | solution.py:60
  85.1 3.9 %fusion.12 = bf16[4,256,256]{1,2,0:T(8,128)(2,1)} fusion(bf16[8,4,168,256]{3,2,1,0:T(8,128)(2,1)} %bitcast.193, bf16[8,168,768]{2,1,0:T(8,128)(2,1)} %bitcast.197), kind=kOutput, calls=%fused_computation.26 | convolution fusion | flops 704905216 | bytes 3964928 | tf_op jit(solution)/shard_map/cfh,cyft->yht/dot_general | solution.py:63
  89.1 27.3 %all-gather.9.cloned.1.call-done = bf16[32,168,256]{2,1,0:T(8,128)(2,1)} async-done(((bf16[4,168,256]{2,1,0:T(8,128)(2,1)}), bf16[32,168,256]{2,1,0:T(8,128)(2,1)}) %all-gather.9.cloned.1.call-update) | async-done | bytes 2752528 | tf_op jit(solution)/shard_map/all_gather | solution.py:59
  116.4 4.8 %fusion.2 = bf16[4,512,256]{1,2,0:T(8,128)(2,1)} fusion(bf16[8,4,168,256]{3,2,1,0:T(8,128)(2,1)} %bitcast.195, bf16[8,168,768]{2,1,0:T(8,128)(2,1)S(1)} %bitcast.199), kind=kOutput, calls=%fused_computation.8 | convolution fusion | flops 1409810432 | bytes 5177344 | tf_op jit(solution)/shard_map/cfh,cyft->yht/dot_general | solution.py:62
  121.3 12.0 %psum.14 = f32[256]{0:T(256)S(1)} all-reduce(f32[256]{0:T(256)S(1)} %get-tuple-element.21), channel_id=1, replica_groups=mesh['z'=8,'y'=4,'x'=4,'k'=2] {'x','k'}, use_global_device_ids=true, to_apply=%region_2.0 | all-reduce | flops 256 | bytes 2048 | tf_op jit(solution)/shard_map/psum | solution.py:46
  133.5 7.9 %reduce-scatter.7.cloned.1.call-done = bf16[1,256,256]{1,2,0:T(8,128)(2,1)} async-done(((bf16[4,256,256]{1,2,0:T(8,128)(2,1)}), bf16[1,256,256]{1,2,0:T(8,128)(2,1)}) %reduce-scatter.7.cloned.1.call-update) | async-done | bytes 131088 | tf_op jit(solution)/shard_map/reduce_scatter | solution.py:65
  142.2 27.6 %reduce-scatter.5.cloned.1.call-done = bf16[1,512,256]{1,2,0:T(8,128)(2,1)} async-done(((bf16[4,512,256]{1,2,0:T(8,128)(2,1)}), bf16[1,512,256]{1,2,0:T(8,128)(2,1)}) %reduce-scatter.5.cloned.1.call-update) | async-done | bytes 262160 | tf_op jit(solution)/shard_map/reduce_scatter | solution.py:64
  172.0 1.3 collective-permute-start.3
  174.1 1.6 collective-permute-start.1
  177.8 2.3 collective-permute-done.2
  180.4 2.7 collective-permute-done.1
  183.4 2.9 collective-permute-done
  190.0 1.6 collective-permute-start.7
  194.0 2.6 collective-permute-start.4
  199.7 1.4 collective-permute-done.4
  203.7 32.4 %all-gather.15.cloned.1.call-done = bf16[3072,256]{0,1:T(8,128)(2,1)} async-done(((bf16[768,256]{0,1:T(8,128)(2,1)}), bf16[3072,256]{0,1:T(8,128)(2,1)}) %all-gather.15.cloned.1.call-update) | async-done | bytes 1572880 | tf_op jit(solution)/shard_map/all_gather | solution.py:117
  236.1 1.7 copy.135
  237.8 4.5 %convert_bitcast_fusion = bf16[8,4,168,256]{3,2,0,1:T(8,128)(2,1)} fusion(bf16[8,168,768]{2,1,0:T(8,128)(2,1)} %bitcast.198, bf16[4,768,256]{2,1,0:T(8,128)(2,1)S(1)} %bitcast.184), kind=kOutput, calls=%fused_computation.1 | convolution fusion | flops 1410662400 | bytes 5177344 | tf_op jit(solution)/shard_map/cfh,yht->cyft/dot_general | solution.py:118
  242.3 2.9 fusion.5
  245.2 1.6 bitcast_convert_fusion
  246.9 1.5 pad_maximum_fusion
  249.6 63.9 %all-reduce.3.cloned.1.call-done = bf16[8,4,168,256]{3,2,0,1:T(8,128)(2,1)} async-done(((bf16[8,4,168,256]{3,2,0,1:T(8,128)(2,1)}), bf16[8,4,168,256]{3,2,0,1:T(8,128)(2,1)}) %all-reduce.3.cloned.1.call-update) | async-done | bytes 2752528
  313.5 2.4 dynamic-slice_bitcast_fusion
  315.9 4.0 %all-to-all-start.2 = ((bf16[4,168,256]{2,1,0:T(8,128)(2,1)}), bf16[4,168,256]{2,1,0:T(8,128)(2,1)S(1)}, u32[]{:S(2)}, u32[]{:S(2)}) async-start(bf16[4,168,256]{2,1,0:T(8,128)(2,1)} %dynamic-slice_bitcast_fusion), calls=%async_computation.4 | async-start | bytes 688128 | tf_op jit(solution)/shard_map/all_to_all | solution.py:120
  319.9 14.6 %psum.15 = f32[256]{0:T(256)S(1)} all-reduce(f32[256]{0:T(256)S(1)} %get-tuple-element.13), channel_id=1, replica_groups=mesh['z'=8,'y'=4,'x'=4,'k'=2] {'x','k'}, use_global_device_ids=true, to_apply=%region_21.22 | all-reduce | flops 256 | bytes 2048 | tf_op jit(solution)/shard_map/psum | solution.py:115
  335.4 20.3 %reduce-scatter.9.cloned.1.call-done = bf16[1,168,768]{2,1,0:T(8,128)(2,1)} async-done(((bf16[8,168,768]{2,1,0:T(8,128)(2,1)}), bf16[1,168,768]{2,1,0:T(8,128)(2,1)}) %reduce-scatter.9.cloned.1.call-update) | async-done | bytes 258064 | tf_op jit(solution)/shard_map/reduce_scatter | solution.py:124
  355.8 1.6 fusion.104
  357.4 1.4 fusion.105
  (117 shorter events, 24.4 us)
Async XLA Ops:
  7.2 16.4 %copy-start = (bf16[256,672]{0,1:T(8,128)(2,1)S(1)}, bf16[256,672]{0,1:T(8,128)(2,1)}, u32[]{:S(2)}) copy-start(bf16[256,672]{0,1:T(8,128)(2,1)} %param.11) | copy-start | bytes 1032196
  7.2 16.4 %copy-start.2 = (f32[672]{0:T(1024)S(1)}, f32[672]{0:T(1024)}, u32[]{:S(2)}) copy-start(f32[672]{0:T(1024)} %param.12) | copy-start | bytes 8068
  7.2 44.3 %all-gather.11.cloned.1.call-start = ((), (), s32[]{:S(2)}) async-start(), calls=%async_computation.10 | async-start | bytes 2322432 | tf_op jit(solution)/shard_map/all_gather | solution.py:61
  9.0 76.1 %all-gather.13.cloned.1.call-start = ((), (), s32[]{:S(2)}) async-start(), calls=%async_computation.11 | async-start | bytes 3096576 | tf_op jit(solution)/shard_map/all_gather | solution.py:60
  23.5 92.9 %all-gather.9.cloned.1.call-start = ((), (), s32[]{:S(2)}) async-start(), calls=%async_computation.9 | async-start | bytes 3096576 | tf_op jit(solution)/shard_map/all_gather | solution.py:59
  32.8 108.5 %reduce-scatter.7.cloned.1.call-start = ((), (), s32[]{:S(2)}) async-start(), calls=%async_computation.7 | async-start | bytes 655360 | tf_op jit(solution)/shard_map/reduce_scatter | solution.py:65
  85.0 31.4 %copy-start.6 = (bf16[1344,768]{1,0:T(8,128)(2,1)S(1)}, bf16[1344,768]{1,0:T(8,128)(2,1)}, u32[]{:S(2)}) copy-start(bf16[1344,768]{1,0:T(8,128)(2,1)} %all-gather.11.cloned.1.call-done) | copy-start | bytes 6193156
  89.0 80.8 %reduce-scatter.5.cloned.1.call-start = ((), (), s32[]{:S(2)}) async-start(), calls=%async_computation.6 | async-start | bytes 1310720 | tf_op jit(solution)/shard_map/reduce_scatter | solution.py:64
  116.4 17.0 %copy-start.4 = (f32[128]{0:T(128)S(1)}, f32[128]{0:T(128)}, u32[]{:S(2)}) copy-start(f32[128]{0:T(128)} %param.13) | copy-start | bytes 1540
  121.2 49.9 %copy-start.3 = (f32[128]{0:T(128)S(1)}, f32[128]{0:T(128)}, u32[]{:S(2)}) copy-start(f32[128]{0:T(128)} %param.14) | copy-start | bytes 1540
  121.2 114.9 %all-gather.15.cloned.1.call-start = ((), (), s32[]{:S(2)}) async-start(), calls=%async_computation.12 | async-start | bytes 1966080 | tf_op jit(solution)/shard_map/all_gather | solution.py:117
  172.0 5.5 %collective-permute-start.3 = (bf16[2,128,256]{1,2,0:T(8,128)(2,1)S(1)}, bf16[2,128,256]{1,2,0:T(8,128)(2,1)S(1)}, u32[]{:S(2)}, u32[]{:S(2)}) collective-permute-start(bf16[2,128,256]{1,2,0:T(8,128)(2,1)S(1)} %pad_maximum_fusion.3), channel_id=1, source_target_pairs={{0,32},{8,40},{16,48},{24,56},{32,64},{40,72},{48,80},{56,88},{64,... | collective-permute-start | bytes 393224 | tf_op jit(solution)/shard_map/ppermute | solution.py:80
  173.4 6.7 %collective-permute-start.2 = (bf16[2,128,256]{1,2,0:T(8,128)(2,1)S(1)}, bf16[2,128,256]{1,2,0:T(8,128)(2,1)S(1)}, u32[]{:S(2)}, u32[]{:S(2)}) collective-permute-start(bf16[2,128,256]{1,2,0:T(8,128)(2,1)S(1)} %pad_maximum_fusion.3), channel_id=1, source_target_pairs={{0,24},{8,32},{16,40},{24,48},{32,56},{40,64},{48,72},{56,80},{64,... | collective-permute-start | bytes 393224 | tf_op jit(solution)/shard_map/ppermute | solution.py:80
  174.1 9.0 %collective-permute-start.1 = (bf16[2,128,256]{1,2,0:T(8,128)(2,1)S(1)}, bf16[2,128,256]{1,2,0:T(8,128)(2,1)S(1)}, u32[]{:S(2)}, u32[]{:S(2)}) collective-permute-start(bf16[2,128,256]{1,2,0:T(8,128)(2,1)S(1)} %pad_maximum_fusion.3), channel_id=1, source_target_pairs={{0,16},{8,24},{16,32},{24,40},{32,48},{40,56},{48,64},{56,72},{64,... | collective-permute-start | bytes 393224 | tf_op jit(solution)/shard_map/ppermute | solution.py:80
  175.7 10.6 %collective-permute-start = (bf16[2,128,256]{1,2,0:T(8,128)(2,1)S(1)}, bf16[2,128,256]{1,2,0:T(8,128)(2,1)S(1)}, u32[]{:S(2)}, u32[]{:S(2)}) collective-permute-start(bf16[2,128,256]{1,2,0:T(8,128)(2,1)S(1)} %pad_maximum_fusion.3), channel_id=1, source_target_pairs={{0,8},{8,16},{16,24},{24,32},{32,40},{40,48},{48,56},{56,64},{64,7... | collective-permute-start | bytes 393224 | tf_op jit(solution)/shard_map/ppermute | solution.py:80
  190.0 8.3 %collective-permute-start.7 = (bf16[2,128,256]{1,2,0:T(8,128)(2,1)S(1)}, bf16[2,128,256]{1,2,0:T(8,128)(2,1)S(1)}, u32[]{:S(2)}, u32[]{:S(2)}) collective-permute-start(bf16[2,128,256]{1,2,0:T(8,128)(2,1)S(1)} %pad_maximum_fusion.8), channel_id=1, source_target_pairs={{0,224},{8,232},{16,240},{24,248},{32,0},{40,8},{48,16},{56,24},{6... | collective-permute-start | bytes 393224 | tf_op jit(solution)/shard_map/ppermute | solution.py:109
  192.0 6.3 %collective-permute-start.6 = (bf16[2,128,256]{1,2,0:T(8,128)(2,1)S(1)}, bf16[2,128,256]{1,2,0:T(8,128)(2,1)S(1)}, u32[]{:S(2)}, u32[]{:S(2)}) collective-permute-start(bf16[2,128,256]{1,2,0:T(8,128)(2,1)S(1)} %pad_maximum_fusion.7), channel_id=1, source_target_pairs={{0,232},{8,240},{16,248},{24,0},{32,8},{40,16},{48,24},{56,32},{64... | collective-permute-start | bytes 393224 | tf_op jit(solution)/shard_map/ppermute | solution.py:109
  192.8 6.9 %collective-permute-start.5 = (bf16[2,128,256]{1,2,0:T(8,128)(2,1)S(1)}, bf16[2,128,256]{1,2,0:T(8,128)(2,1)S(1)}, u32[]{:S(2)}, u32[]{:S(2)}) collective-permute-start(bf16[2,128,256]{1,2,0:T(8,128)(2,1)S(1)} %pad_maximum_fusion.6), channel_id=1, source_target_pairs={{0,240},{8,248},{16,0},{24,8},{32,16},{40,24},{48,32},{56,40},{64,... | collective-permute-start | bytes 393224 | tf_op jit(solution)/shard_map/ppermute | solution.py:109
  194.0 7.0 %collective-permute-start.4 = (bf16[2,128,256]{1,2,0:T(8,128)(2,1)S(1)}, bf16[2,128,256]{1,2,0:T(8,128)(2,1)S(1)}, u32[]{:S(2)}, u32[]{:S(2)}) collective-permute-start(bf16[2,128,256]{1,2,0:T(8,128)(2,1)S(1)} %pad_maximum_fusion.5), channel_id=1, source_target_pairs={{0,248},{8,0},{16,8},{24,16},{32,24},{40,32},{48,40},{56,48},{64,5... | collective-permute-start | bytes 393224 | tf_op jit(solution)/shard_map/ppermute | solution.py:109
  201.1 1.5 copy-start.1
  203.7 109.8 %all-reduce.3.cloned.1.call-start = ((), (), s32[]{:S(2)}) async-start(), calls=%async_computation.13 | async-start | bytes 5505024
  242.3 113.5 %reduce-scatter.9.cloned.1.call-start = ((), (), s32[]{:S(2)}) async-start(), calls=%async_computation.8 | async-start | bytes 2322432 | tf_op jit(solution)/shard_map/reduce_scatter | solution.py:124
  242.3 2.9 copy-start.5
  248.3 0.7 copy-start.7
  315.9 18.6 %all-to-all-start.2 = ((bf16[4,168,256]{2,1,0:T(8,128)(2,1)}), bf16[4,168,256]{2,1,0:T(8,128)(2,1)S(1)}, u32[]{:S(2)}, u32[]{:S(2)}) async-start(bf16[4,168,256]{2,1,0:T(8,128)(2,1)} %dynamic-slice_bitcast_fusion), calls=%async_computation.4 | async-start | bytes 688128 | tf_op jit(solution)/shard_map/all_to_all | solution.py:120
Sparse Core Ops, SparseCore 0:
  10.4 41.1 all-gather.10
  53.4 31.6 all-gather.12
  86.9 29.4 all-gather.8
  118.8 22.4 reduce-scatter.6
  143.7 26.0 reduce-scatter.4
  203.8 32.2 all-gather.14
  242.4 71.0 all-reduce.2
  316.1 39.6 reduce-scatter.8

commit v2 on v1

v2 whole, which is shorter than its diff:
```python
import jax
import jax.numpy as jnp
from jax import lax
from jax.experimental import pallas as pl
from jax.experimental.pallas import tpu as pltpu
from jax.sharding import Mesh
from jax.sharding import PartitionSpec as P

D = 5376
HD = 128
WIN = 1024
NZ, NY, NX, NK = 8, 4, 4, 2
NC = NX * NK
TOK = 256
FR = 168
NDOC = 8
NSEM = 240
epsilon = 1e-06
query_scale = 168.0 ** (-0.5)
f32 = jnp.float32
bf16 = jnp.bfloat16
MESH = pl.DeviceIdType.MESH


def dot(a, b, ca, cb):
    return lax.dot_general(a, b, (((ca,), (cb,)), ((), ())), preferred_element_type=f32)


def eye(n):
    return (lax.broadcasted_iota(jnp.int32, (n, n), 0) == lax.broadcasted_iota(jnp.int32, (n, n), 1)).astype(bf16)


def rot(v, c, s):
    a, b = v[: HD // 2], v[HD // 2 :]
    return jnp.concatenate([a * c - b * s, b * c + a * s], 0)


def unit(p):
    sc = lax.rsqrt(jnp.mean(p * p, 0, keepdims=True) + epsilon)
    return p * sc, sc


def unit_back(w, u, sc):
    return sc * (w - u * jnp.mean(w * u, 0, keepdims=True))


def kernel(
    tokens, upstream, gain, q_gain, k_gain, wq, wk, wv, wo, cos_t, sin_t, docs, labels,
    g_in, g_wq, g_wk, g_wv, g_wo,
    xsrc, csrc, X, C, Wp, Wo, ssq, inn, raw,
    pq, pr, prh, oq, orr, orh,
    KV, ex, dsb, drb, A, Gq, Gk,
    hb, hr, sb, rb,
    nb, nr, mh, mrh, mb, mr, ds_, dr_, dn,
    sem_s, sem_r,
):
    z, y, x, k = (lax.axis_index(n) for n in ("z", "y", "x", "k"))
    c = x * NK + k
    row = z * NY + y
    zi = [lax.rem(z + r, NZ) for r in range(NZ)]
    yi = [lax.rem(y + r, NY) for r in range(NY)]
    xi = [lax.rem(x + r, NX) for r in range(NX)]
    ko = 1 - k
    rows = {}
    for d in (1, 2, 3, 4, -1, -2, -3, -4):
        rr = lax.rem(row + d + NZ * NY, NZ * NY)
        rows[d] = {"z": rr // NY, "y": lax.rem(rr, NY)}
    cols = []
    for d in range(1, NC):
        cc = lax.rem(c + d, NC)
        cols.append({"x": cc // NK, "k": lax.rem(cc, NK)})

    barrier = pltpu.get_barrier_semaphore()
    for dev in list(rows.values()) + cols:
        pl.semaphore_signal(barrier, inc=1, device_id=dev, device_id_type=MESH)

    count = [0]
    started = []

    def send(src, dst, dev):
        i = count[0]
        count[0] += 1
        copy = pltpu.make_async_remote_copy(
            src_ref=src, dst_ref=dst, send_sem=sem_s.at[i], recv_sem=sem_r.at[i],
            device_id=dev, device_id_type=MESH,
        )
        copy.start()
        started.append(copy)
        return copy

    zp, zm = {"z": zi[1]}, {"z": zi[NZ - 1]}
    yp, ym = {"y": yi[1]}, {"y": yi[NY - 1]}
    xp, xm = {"x": xi[1]}, {"x": xi[NX - 1]}
    sib = {"k": ko}

    Wp[z, :, 0:256] = wq[...]
    Wp[z, :, 256:384] = wk[...]
    Wp[z, :, 384:512] = wv[...]
    Wo[z] = wo[...]
    pl.semaphore_wait(barrier, len(rows) + len(cols))

    def ring_start(W):
        return [send(W.at[z], W.at[z], zp)], [send(W.at[z], W.at[z], zm)]

    def ring_step(W, fwd, bwd, half):
        s = len(fwd)
        zf, zb = zi[NZ - s], zi[s]
        fwd[-1].wait_recv()
        if s < 3:
            fwd.append(send(W.at[zf], W.at[zf], zp))
        elif s == 3:
            fwd.append(send(W.at[zf, :, pl.ds(0, half)], W.at[zf, :, pl.ds(0, half)], zp))
        bwd[-1].wait_recv()
        if s < 3:
            bwd.append(send(W.at[zb], W.at[zb], zm))
        elif s == 3:
            bwd.append(send(W.at[zb, :, pl.ds(half, half)], W.at[zb, :, pl.ds(half, half)], zm))

    ring_p = ring_start(Wp)

    raw[...] = dot(eye(NY * FR), tokens[...], 1, 1)
    x32 = raw[...]
    own_sq = jnp.sum(x32 * x32, 0, keepdims=True)
    ssq[c] = jnp.broadcast_to(own_sq, (8, TOK))
    for i in range(NY):
        xsrc[i] = (raw[i * FR : (i + 1) * FR] * gain[i * FR : (i + 1) * FR]).astype(bf16)

    def exchange(src, Y):
        out = {}
        for e in (2, 1, 3):
            out[e] = send(src.at[yi[e]], Y.at[c, y], {"y": yi[e]})
        Y[c, y] = src[yi[0]]
        return out

    a2x = exchange(xsrc, X)

    def spread(Y, e, far):
        ref = Y.at[c, yi[e]]
        far["p", e] = send(ref, ref, xp)
        far["m", e] = send(ref, ref, xm)
        far["s", 0, e] = send(ref, ref, sib)

    def onward(Y, e, far):
        left = Y.at[xi[NX - 1] * NK + k, yi[e]]
        right = Y.at[xi[1] * NK + k, yi[e]]
        far["p", e].wait_recv()
        if e in (0, 1):
            far["f", e] = send(left, left, xp)
        far["s", 1, e] = send(left, left, sib)
        far["m", e].wait_recv()
        if e in (2, 3):
            far["f", e] = send(right, right, xm)
        far["s", 2, e] = send(right, right, sib)

    def across(Y, e, far):
        ref = Y.at[xi[2] * NK + k, yi[e]]
        far["f", e].wait_recv()
        far["s", 3, e] = send(ref, ref, sib)

    def gathered(far):
        for i in range(4):
            for e in range(NY):
                far["s", i, e].wait_recv()

    fx, fc = {}, {}
    spread(X, 0, fx)
    sq_sent = [send(ssq.at[c], ssq.at[c], dev) for dev in cols]

    own_docs = docs[pl.ds(row, 1), :].astype(f32)
    all_docs = docs[...].astype(f32)
    sign = jnp.ones((1, TOK), f32)
    start = jnp.zeros((1, TOK), f32)
    for d in range(NDOC):
        member = (own_docs == d).astype(f32)
        sign = sign - 2.0 * member * labels[d].astype(f32)
        start = start + member * jnp.sum(
            jnp.sum((all_docs < d).astype(f32), 0, keepdims=True), 1, keepdims=True
        )
    lane = lax.broadcasted_iota(jnp.int32, (1, TOK), 1).astype(f32)
    low = jnp.maximum(start - (row * TOK).astype(f32), lane - (WIN - 1.0))
    up_t = dot(eye(NY * FR), upstream[...], 1, 1)
    for i in range(NY):
        csrc[i] = (up_t[i * FR : (i + 1) * FR] * sign).astype(bf16)

    for e in (1, 3):
        a2x[4 - e].wait_recv()
        spread(X, e, fx)
    ring_step(Wp, *ring_p, 256)
    a2x[2].wait_recv()
    spread(X, 2, fx)
    a2c = exchange(csrc, C)
    onward(X, 0, fx)
    onward(X, 1, fx)
    ring_step(Wp, *ring_p, 256)
    onward(X, 3, fx)
    onward(X, 2, fx)
    ring_step(Wp, *ring_p, 256)
    ring_o = ring_start(Wo)
    for e in (0, 1, 3):
        across(X, e, fx)
    spread(C, 0, fc)
    across(X, 2, fx)
    for e in (1, 3, 2):
        a2c[4 - e].wait_recv()
        spread(C, e, fc)
    gathered(fx)
    ring_step(Wp, *ring_p, 256)

    def partial(W, Y, e):
        total = None
        for i in range(NC):
            t = dot(W[i], Y[i, yi[e]], 0, 0)
            total = t if total is None else total + t
        return total

    def reduce_far(W, Y, buf, got, n):
        buf[0] = partial(W, Y, 2).astype(bf16)
        h = n // 2
        return (
            send(buf.at[0, pl.ds(0, h)], got.at[0], yp),
            send(buf.at[0, pl.ds(h, h)], got.at[1], ym),
        )

    def reduce_near(W, Y, buf, got, full, n, sent):
        h = n // 2
        t = partial(W, Y, 1)
        sent[0].wait_recv()
        buf[1, 0:h] = (t[0:h] + got[0].astype(f32)).astype(bf16)
        buf[1, h:n] = t[h:n].astype(bf16)
        a = send(buf.at[1], full.at[0], yp)
        t = partial(W, Y, 3)
        sent[1].wait_recv()
        buf[2, 0:h] = t[0:h].astype(bf16)
        buf[2, h:n] = (t[h:n] + got[1].astype(f32)).astype(bf16)
        b = send(buf.at[2], full.at[1], ym)
        return a, b

    far_q = reduce_far(Wp, X, pq, prh, 512)
    onward(C, 0, fc)
    near_q = reduce_near(Wp, X, pq, prh, pr, 512, far_q)
    ring_step(Wo, *ring_o, 128)
    onward(C, 1, fc)
    onward(C, 3, fc)
    own_q = partial(Wp, X, 0)
    ring_step(Wo, *ring_o, 128)
    onward(C, 2, fc)
    for s in sq_sent:
        s.wait_recv()
    total_sq = ssq[0, 0:1]
    for i in range(1, NC):
        total_sq = total_sq + ssq[i, 0:1]
    scale = lax.rsqrt(total_sq / D + epsilon)
    near_q[0].wait_recv()
    near_q[1].wait_recv()
    proj = (own_q + pr[0].astype(f32) + pr[1].astype(f32)) * scale
    co, si = cos_t[...], sin_t[...]
    qg, kg = q_gain[...], k_gain[...]
    uq0, sq0 = unit(proj[0:128])
    uq1, sq1 = unit(proj[128:256])
    uk, sk = unit(proj[256:384])
    q = jnp.concatenate([rot(uq0 * qg, co, si), rot(uq1 * qg, co, si)], 1) * query_scale
    q = q.astype(bf16)
    KV[0, 0:128] = rot(uk * kg, co, si).astype(bf16)
    KV[0, 128:256] = proj[384:512].astype(bf16)
    kv_sent = {d: send(KV.at[0], KV.at[d], rows[d]) for d in (4, 1, 2, 3)}
    ring_step(Wo, *ring_o, 128)
    for e in (0, 1, 3, 2):
        across(C, e, fc)
    ring_step(Wo, *ring_o, 128)
    gathered(fc)
    far_o = reduce_far(Wo, C, oq, orh, 256)
    near_o = reduce_near(Wo, C, oq, orh, orr, 256, far_o)
    own_o = partial(Wo, C, 0)

    low2 = jnp.concatenate([low, low], 1)
    at2 = jnp.concatenate([lane, lane], 1)
    below = lax.broadcasted_iota(jnp.int32, (TOK, 2 * TOK), 0).astype(f32)
    total = jnp.zeros((1, 2 * TOK), f32)
    attn = jnp.zeros((HD, 2 * TOK), f32)
    for d in (0, 1, 4, 3, 2):
        if d:
            kv_sent[d].wait_recv()
        s = dot(KV[d, 0:128], q, 0, 0)
        ok = below >= low2 + d * TOK
        if d == 0:
            ok = ok & (below <= at2)
        e = jnp.where(ok, jnp.exp(s), 0.0)
        ex[d] = e
        total = total + jnp.sum(e, 0, keepdims=True)
        attn = attn + dot(KV[d, 128:256], e.astype(bf16), 1, 0)
    inv = 1.0 / total
    attn = attn * inv
    A[y, 0:128] = attn[:, 0:TOK].astype(bf16)
    A[y, 128:256] = attn[:, TOK:].astype(bf16)

    def ag_start(B):
        return [send(B.at[y], B.at[y], yp), send(B.at[y], B.at[y], ym)]

    def ag_step(B, s):
        s[0].wait_recv()
        low_half = B.at[yi[3], pl.ds(0, 128)]
        s.append(send(low_half, low_half, yp))
        s[1].wait_recv()
        high_half = B.at[yi[1], pl.ds(128, 128)]
        s.append(send(high_half, high_half, ym))

    def ag_end(s):
        s[2].wait_recv()
        s[3].wait_recv()

    ag_a = ag_start(A)
    near_o[0].wait_recv()
    near_o[1].wait_recv()
    da = own_o + orr[0].astype(f32) + orr[1].astype(f32)
    da = jnp.concatenate([da[0:128], da[128:256]], 1).astype(bf16)
    delta = jnp.sum(attn * da.astype(f32), 0, keepdims=True)
    dq = jnp.zeros((HD, 2 * TOK), f32)
    dkv_sent = {}
    for d in (4, 2, 3, 1, 0):
        p = ex[d] * inv
        dp = dot(KV[d, 128:256], da, 0, 0)
        ds = (p * (dp - delta)).astype(bf16)
        dq = dq + dot(KV[d, 0:128], ds, 1, 0)
        dk = dot(q, ds, 1, 1)
        dv = dot(da, p.astype(bf16), 1, 1)
        if d:
            dsb[d - 1, 0:128] = dk.astype(bf16)
            dsb[d - 1, 128:256] = dv.astype(bf16)
            dkv_sent[d] = send(dsb.at[d - 1], drb.at[d - 1], rows[-d])
    ag_step(A, ag_a)
    g0 = unit_back(rot(dq[:, 0:TOK], co, -si) * query_scale * qg, uq0, sq0) * scale
    g1 = unit_back(rot(dq[:, TOK:], co, -si) * query_scale * qg, uq1, sq1) * scale
    Gq[y, 0:128] = g0.astype(bf16)
    Gq[y, 128:256] = g1.astype(bf16)
    ag_q = ag_start(Gq)
    ag_end(ag_a)

    def whole(B, i):
        return jnp.concatenate([B[i, j] for j in range(NY)], 1)

    stores = [(C, A), (X, Gq), (X, Gk)]

    def part(u, r):
        L, B = stores[u]
        right = jnp.concatenate([B[j] for j in range(NY)], 1)
        return dot(whole(L, zi[r % NZ]), right, 1, 1)

    zc = {}

    def zs0(u):
        t = part(u, 4).astype(bf16)
        hb[u, 0] = t[:, 0:128]
        hb[u, 1] = t[:, 128:256]
        zc[u, 0, 0] = send(hb.at[u, 0], hr.at[u, 0], zp)
        zc[u, 1, 0] = send(hb.at[u, 1], hr.at[u, 1], zm)

    def zs1(u):
        t = part(u, 3)
        zc[u, 0, 0].wait_recv()
        sb[u, 0, 0, :, 0:128] = (t[:, 0:128] + hr[u, 0].astype(f32)).astype(bf16)
        sb[u, 0, 0, :, 128:256] = t[:, 128:256].astype(bf16)
        zc[u, 0, 1] = send(sb.at[u, 0, 0], rb.at[u, 0, 0], zp)
        t = part(u, -3)
        zc[u, 1, 0].wait_recv()
        sb[u, 1, 0, :, 0:128] = t[:, 0:128].astype(bf16)
        sb[u, 1, 0, :, 128:256] = (t[:, 128:256] + hr[u, 1].astype(f32)).astype(bf16)
        zc[u, 1, 1] = send(sb.at[u, 1, 0], rb.at[u, 1, 0], zm)

    def zsn(u, n):
        for w, (sgn, dev) in enumerate(((1, zp), (-1, zm))):
            t = part(u, sgn * (4 - n))
            zc[u, w, n - 1].wait_recv()
            sb[u, w, n - 1] = (t + rb[u, w, n - 2].astype(f32)).astype(bf16)
            zc[u, w, n] = send(sb.at[u, w, n - 1], rb.at[u, w, n - 1], dev)

    def zs4(u):
        t = part(u, 0)
        zc[u, 0, 3].wait_recv()
        zc[u, 1, 3].wait_recv()
        return (t + rb[u, 0, 2].astype(f32) + rb[u, 1, 2].astype(f32)).astype(bf16)

    zs0(0)
    ag_step(Gq, ag_q)
    for d in (1, 3, 2, 4):
        dkv_sent[d].wait_recv()
    for d in (1, 3, 2, 4):
        dk = dk + drb[d - 1, 0:128].astype(f32)
        dv = dv + drb[d - 1, 128:256].astype(f32)
    gk = unit_back(rot(dk, co, -si) * kg, uk, sk) * scale
    gv = dv * scale
    Gk[y, 0:128] = gk.astype(bf16)
    Gk[y, 128:256] = gv.astype(bf16)
    ag_k = ag_start(Gk)
    inner = jnp.sum(
        g0 * proj[0:128] + g1 * proj[128:256] + gk * proj[256:384] + gv * proj[384:512], 0, keepdims=True
    )
    inn[c] = jnp.broadcast_to(inner, (8, TOK))
    in_sent = [send(inn.at[c], inn.at[c], dev) for dev in cols]
    zs1(0)
    ag_end(ag_q)
    zs0(1)
    ag_step(Gk, ag_k)
    zsn(0, 2)
    zs1(1)
    ag_end(ag_k)

    def share(i, j):
        g = jnp.concatenate([Gq[j], Gk[j]], 0)
        return dot(Wp[i], g, 1, 0)

    nc = {}
    for r in (2, 1, 3, 0):
        for j in range(NY):
            nb[r, j] = share(xi[r] * NK + ko, j).astype(bf16)
        nc[r] = send(nb.at[r], nr.at[r], sib)
    zs0(2)
    zsn(0, 3)
    nc[2].wait_recv()
    for j in range(NY):
        mh[j] = (share(xi[2] * NK + k, j) + nr[2, j].astype(f32)).astype(bf16)
    xf = send(mh.at[pl.ds(0, 2)], mrh.at[0], xp)
    xb = send(mh.at[pl.ds(2, 2)], mrh.at[1], xm)
    zsn(1, 2)
    zs1(2)
    nc[1].wait_recv()
    nc[3].wait_recv()
    mid = {}
    for w, r in enumerate((1, 3)):
        (xf, xb)[w].wait_recv()
        for j in range(NY):
            t = share(xi[r] * NK + k, j) + nr[r, j].astype(f32)
            if j // 2 == w:
                t = t + mrh[w, j % 2].astype(f32)
            mb[w, j] = t.astype(bf16)
        mid[w] = send(mb.at[w], mr.at[w], (xp, xm)[w])
    g_wo[...] = zs4(0)
    zsn(1, 3)
    zsn(2, 2)
    nc[0].wait_recv()
    mid[0].wait_recv()
    mid[1].wait_recv()
    for j in range(NY):
        t = share(xi[0] * NK + k, j) + nr[0, j].astype(f32)
        ds_[j] = (t + mr[0, j].astype(f32) + mr[1, j].astype(f32)).astype(bf16)
    dr_[y] = ds_[y]
    back = [send(ds_.at[yi[e]], dr_.at[y], {"y": yi[e]}) for e in (2, 1, 3)]
    zsn(2, 3)
    g_wq[...] = zs4(1)
    for s in in_sent:
        s.wait_recv()
    in_total = inn[0, 0:1]
    for i in range(1, NC):
        in_total = in_total + inn[i, 0:1]
    factor = scale * in_total / D
    for s in back:
        s.wait_recv()
    for j in range(NY):
        here = slice(j * FR, (j + 1) * FR)
        dn[here] = dr_[j].astype(f32) * gain[here] - raw[here] * factor
    g_in[...] = dot(eye(TOK), dn[...].astype(bf16), 1, 1).astype(bf16)
    last = zs4(2)
    g_wk[...] = last[:, 0:128]
    g_wv[...] = last[:, 128:256]
    for s in started:
        s.wait_send()


def tables(row):
    half = HD // 2
    positions = (row * TOK + jnp.arange(TOK, dtype=jnp.int32)).astype(f32)
    frequency = 10000.0 ** (-(2.0 * jnp.arange(half, dtype=f32)) / HD)
    angles = frequency[:, None] * positions[None, :]
    return jnp.cos(angles), jnp.sin(angles)


def per_device(tokens, input_gain, q_gain, k_gain, wq, wk, wv, wo, upstream, doc_ids, doc_labels):
    row = lax.axis_index("z") * NY + lax.axis_index("y")
    cos_t, sin_t = tables(row)
    V = pltpu.VMEM
    piece = (FR, TOK)
    scratch = [
        V((NY,) + piece, bf16), V((NY,) + piece, bf16),
        V((NC, NY) + piece, bf16), V((NC, NY) + piece, bf16),
        V((NZ, FR, 512), bf16), V((NZ, FR, 256), bf16),
        V((NC, 8, TOK), f32), V((NC, 8, TOK), f32), V((NY * FR, TOK), f32),
        V((3, 512, TOK), bf16), V((2, 512, TOK), bf16), V((2, 256, TOK), bf16),
        V((3, 256, TOK), bf16), V((2, 256, TOK), bf16), V((2, 128, TOK), bf16),
        V((5, 256, TOK), bf16), V((5, TOK, 2 * TOK), f32),
        V((4, 256, TOK), bf16), V((4, 256, TOK), bf16),
        V((NY, 256, TOK), bf16), V((NY, 256, TOK), bf16), V((NY, 256, TOK), bf16),
        V((3, 2, FR, 128), bf16), V((3, 2, FR, 128), bf16),
        V((3, 2, 3, FR, 256), bf16), V((3, 2, 3, FR, 256), bf16),
        V((NX, NY) + piece, bf16), V((NX, NY) + piece, bf16),
        V((NY,) + piece, bf16), V((2, 2) + piece, bf16),
        V((2, NY) + piece, bf16), V((2, NY) + piece, bf16),
        V((NY,) + piece, bf16), V((NY,) + piece, bf16), V((NY * FR, TOK), f32),
        pltpu.SemaphoreType.DMA((NSEM,)), pltpu.SemaphoreType.DMA((NSEM,)),
    ]
    vm = pl.BlockSpec(memory_space=pltpu.VMEM)
    out = [
        jax.ShapeDtypeStruct((TOK, NY * FR), bf16),
        jax.ShapeDtypeStruct((FR, 256), bf16),
        jax.ShapeDtypeStruct((FR, 128), bf16),
        jax.ShapeDtypeStruct((FR, 128), bf16),
        jax.ShapeDtypeStruct((FR, 256), bf16),
    ]
    return pl.pallas_call(
        kernel,
        out_shape=out,
        in_specs=[vm] * 12 + [pl.BlockSpec(memory_space=pltpu.SMEM)],
        out_specs=[vm] * 5,
        scratch_shapes=scratch,
        compiler_params=pltpu.CompilerParams(
            collective_id=0, has_side_effects=True, vmem_limit_bytes=60 * 1024 * 1024
        ),
    )(
        tokens, upstream, input_gain[:, None], q_gain[:, None], k_gain[:, None], wq, wk, wv, wo,
        cos_t, sin_t, doc_ids.reshape(NZ * NY, TOK), doc_labels,
    )


def solution(mesh):
    fine = Mesh(mesh.devices.reshape(NZ, NY, NX, NK), ("z", "y", "x", "k"))
    rc = P(("z", "y"), ("x", "k"))
    return jax.shard_map(
        per_device,
        mesh=fine,
        in_specs=(rc, P(("x", "k")), P(), P(), rc, rc, rc, rc, rc, P(), P()),
        out_specs=(rc,) * 5,
        check_vma=False,
    )
```

time: 369 us -> 132 us (0.36)
  waiting for transfers between devices: 243 us -> 0 us
  Pallas kernels: 0 us -> 118 us
  blocking collectives: 46.6 us -> 0 us
  matrix products: 25.4 us -> 0 us
  between operations: 14.7 us -> 0.71 us
  starting transfers between devices: 13.9 us -> 0 us
  other arithmetic: 12 us -> 0.98 us
    pallas_call x0 -> x1, Pallas kernels: none -> 118 us  [per_device(): pl.pallas_call(kernel, out_shape=out, in_specs=[vm] * 12 + [pl.BlockSpec(...]
    all_gather x4 -> x0, waiting for transfers between devices: 112 us -> none  [the longest x1 33.5 us: per_device(): C = lax.all_gather(ca, col)]
    unnamed x9 -> x0, waiting for transfers between devices: 64 us -> none
    reduce_scatter x3 -> x0, waiting for transfers between devices: 55.8 us -> none  [the longest x1 27.6 us: per_device(): proj = lax.psum_scatter(qkv, 'y', scatter_dimension=0).astype(f32) * scale]
    psum x2 -> x0, blocking collectives: 26.6 us -> none  [the longest x1 14.6 us: per_device(): inner = lax.psum(jnp.sum(G * proj, 0), col) / D]
    dot_general x35 -> x0, matrix products: 25.4 us -> none  [the longest x1 4.79 us: per_device(): jnp.einsum('cfh,cyft->yht', W[:, :, :512], X, preferred_element_type=f32)]
    all_to_all x2 -> x0, blocking collectives: 20 us -> none  [the longest x1 10.9 us: per_device(): ca = lax.all_to_all(ct, 'y', 0, 0)]
    ppermute x8 -> x0, waiting for transfers between devices: 11.2 us -> none  [the longest x4 8.48 us: per_device(): blocks.append(lax.ppermute(kv, ('z', 'y'), route))]
  transfers between devices with their start and end apart: 17 -> 0, of which waited for: 14 -> 0; matrix products, arithmetic and copies ran while one was open for 8% -> 0% of each run, Pallas kernels for 0% -> 0%
where the time goes in v2:
time: 132 us; the launch traced here: 130 us
  Pallas kernels  118 us (89%)
  local copies, waits for them, and re-layouts  10.3 us (8%)
    pallas_call x1, Pallas kernels, per_device(): pl.pallas_call(kernel, out_shape=out, in_specs=[vm] * 12 + [pl.BlockSpec(...  118 us
    unnamed x24, local copies, waits for them, and re-layouts  4.57 us

profile of v2, /device:TPU:1, one launch (start us, length us, event | category | flops | bytes accessed | tf_op | source)
XLA Modules:
  0.0 129.8 jit_solution(1155068636839254350)
XLA Ops:
  0.6 0.0 copy-start.7
  0.6 0.0 copy-start.8
  0.7 0.0 copy-start.6
  0.7 0.0 copy-start
  0.7 1.4 %reshape.25.docs = s32[32,256]{1,0:T(8,128)} reshape(s32[8192]{0:T(1024)} %param.20) | data formatting | bytes 65536 | tf_op jit(solution)/shard_map/reshape | solution.py:518
  2.1 0.0 copy-done.7
  2.1 0.7 copy.24.q_gain
  2.9 0.0 copy-done.8
  2.9 0.7 copy.25.k_gain
  3.6 1.0 multiply_sine_fusion
  4.6 0.0 copy-done.6
  4.6 0.9 broadcast_in_dim.14.gain
  5.5 0.0 copy-done
  5.5 0.0 copy-start.1
  5.5 0.9 copy.21.tokens
  6.4 0.1 copy-done.1
  6.5 0.9 copy.22.upstream
  7.4 117.8 %shard_map.146 = (bf16[256,672]{1,0:T(8,128)(2,1)}, bf16[168,256]{1,0:T(8,128)(2,1)}, bf16[168,128]{1,0:T(8,128)(2,1)}, bf16[168,128]{1,0:T(8,128)(2,1)}, bf16[168,256]{1,0:T(8,128)(2,1)}) custom-call(bf16[256,672]{1,0:T(8,128)(2,1)} %copy.21.tokens, bf16[256,672]{1,0:T(8,128)(2,1)} %copy.22.upstream, f32[672,1]{1,0:T(8,128)} %broadcast_in_dim.14.gain, ...), custom_call_target="tpu_custom_call" | custom-call | tf_op jit(solution)/shard_map/pallas_call | solution.py:507
  125.1 0.0 copy-start.3
  125.2 1.9 %copy.26 = bf16[256,672]{0,1:T(8,128)(2,1)} copy(bf16[256,672]{1,0:T(8,128)(2,1)} %get-tuple-element.10) | data formatting | bytes 688128 | tf_op jit(solution)/shard_map/pallas_call | solution.py:507
  127.1 0.0 copy-done.3
  127.1 0.0 copy-start.5
  127.1 0.0 copy-start.4
  127.1 0.6 copy.31
  127.7 0.1 copy-done.5
  127.9 0.0 copy-start.2
  127.9 0.6 copy.32
  128.5 0.0 copy-done.4
  128.5 0.6 copy.33
  129.1 0.0 copy-done.2
  129.1 0.6 copy.34
  (2 shorter events, 0.0 us)
Async XLA Ops:
  0.6 1.5 %copy-start.7 = (f32[128]{0:T(128)S(1)}, f32[128]{0:T(128)}, u32[]{:S(2)}) copy-start(f32[128]{0:T(128)} %param.13) | copy-start | bytes 1540
  0.6 2.2 %copy-start.8 = (f32[128]{0:T(128)S(1)}, f32[128]{0:T(128)}, u32[]{:S(2)}) copy-start(f32[128]{0:T(128)} %param.14) | copy-start | bytes 1540
  0.7 3.9 %copy-start.6 = (f32[672]{0:T(1024)S(1)}, f32[672]{0:T(1024)}, u32[]{:S(2)}) copy-start(f32[672]{0:T(1024)} %param.12) | copy-start | bytes 8068
  0.7 4.8 %copy-start = (bf16[256,672]{0,1:T(8,128)(2,1)S(1)}, bf16[256,672]{0,1:T(8,128)(2,1)}, u32[]{:S(2)}) copy-start(bf16[256,672]{0,1:T(8,128)(2,1)} %param.11) | copy-start | bytes 1032196
  5.5 1.0 copy-start.1
  125.1 1.9 %copy-start.3 = (bf16[168,256]{1,0:T(8,128)(2,1)S(1)}, bf16[168,256]{1,0:T(8,128)(2,1)}, u32[]{:S(2)}) copy-start(bf16[168,256]{1,0:T(8,128)(2,1)} %get-tuple-element.23) | copy-start | bytes 258052
  127.1 0.8 copy-start.5
  127.1 1.4 %copy-start.4 = (bf16[168,128]{1,0:T(8,128)(2,1)S(1)}, bf16[168,128]{1,0:T(8,128)(2,1)}, u32[]{:S(2)}) copy-start(bf16[168,128]{1,0:T(8,128)(2,1)} %get-tuple-element.25) | copy-start | bytes 129028
  127.9 1.2 copy-start.2

commit v3 on v2

v3 whole, which is shorter than its diff:
```python
import math

import jax
import jax.numpy as jnp
from jax import lax
from jax.experimental import pallas as pl
from jax.experimental.pallas import tpu as pltpu
from jax.sharding import Mesh
from jax.sharding import PartitionSpec as P

D = 5376
HD = 128
WIN = 1024
NZ, NY, NX, NK = 8, 4, 4, 2
NC = NX * NK
TOK = 256
FR = 168
NDOC = 8
NSEM = 256
epsilon = 1e-06
query_scale = 168.0 ** (-0.5)
f32 = jnp.float32
bf16 = jnp.bfloat16
MESH = pl.DeviceIdType.MESH


def dot(a, b, ca, cb):
    return lax.dot_general(a, b, (((ca,), (cb,)), ((), ())), preferred_element_type=f32)


def rot(v, c, s):
    a, b = v[: HD // 2], v[HD // 2 :]
    return jnp.concatenate([a * c - b * s, b * c + a * s], 0)


def unit(p):
    sc = lax.rsqrt(jnp.mean(p * p, 0, keepdims=True) + epsilon)
    return p * sc, sc


def unit_back(w, u, sc):
    return sc * (w - u * jnp.mean(w * u, 0, keepdims=True))


def column(v):
    n = v.shape[1]
    parts = []
    for i in range(0, n, 128):
        w = min(128, n - i)
        same = lax.broadcasted_iota(jnp.int32, (w, w), 0) == lax.broadcasted_iota(jnp.int32, (w, w), 1)
        parts.append(jnp.sum(jnp.where(same, v[:, i : i + w], 0.0), 1, keepdims=True))
    return jnp.concatenate(parts, 0) if len(parts) > 1 else parts[0]


def kernel(
    tokens, upstream, gain, q_gain, k_gain, wq, wk, wv, wo, docs_in, labels,
    g_in, g_wq, g_wk, g_wv, g_wo,
    tok, ups, g_row, qg_row, kg_row, docs,
    xsrc, csrc, X, C, Wp, Wo, ssq, inn, gcol, cs,
    pq, pr, prh,
    KV, ex, dsb, drb, A, Gq, Gk,
    hb, hr, sb, rb,
    nb, nr, mh, mrh, mb, mr, ds_, dr_,
    sem_l, sem_s, sem_r,
):
    z, y, x, k = (lax.axis_index(n) for n in ("z", "y", "x", "k"))
    c = x * NK + k
    row = z * NY + y
    zi = [lax.rem(z + r, NZ) for r in range(NZ)]
    yi = [lax.rem(y + r, NY) for r in range(NY)]
    xi = [lax.rem(x + r, NX) for r in range(NX)]
    ko = 1 - k
    zp, zm = {"z": zi[1]}, {"z": zi[NZ - 1]}
    yp, ym = {"y": yi[1]}, {"y": yi[NY - 1]}
    xp, xm = {"x": xi[1]}, {"x": xi[NX - 1]}
    sib = {"k": ko}
    cols = []
    for d in range(1, NC):
        cc = lax.rem(c + d, NC)
        cols.append({"x": cc // NK, "k": lax.rem(cc, NK)})

    barrier = pltpu.get_barrier_semaphore()
    peers = [zp, zm, yp, ym, {"y": yi[2]}] + cols
    for dev in peers:
        pl.semaphore_signal(barrier, inc=1, device_id=dev, device_id_type=MESH)

    loads = []
    for n, (src, dst) in enumerate((
        (wq, Wp.at[z, :, pl.ds(0, 256)]), (wk, Wp.at[z, :, pl.ds(256, 128)]), (wv, Wp.at[z, :, pl.ds(384, 128)]),
        (tokens, tok), (gain, g_row), (docs_in, docs), (upstream, ups), (wo, Wo.at[z]), (q_gain, qg_row), (k_gain, kg_row),
    )):
        loads.append(pltpu.make_async_copy(src, dst, sem_l.at[n]))
        loads[-1].start()

    count = [0]
    started = []

    def make(src, dst, dev, i):
        return pltpu.make_async_remote_copy(
            src_ref=src, dst_ref=dst, send_sem=sem_s.at[i], recv_sem=sem_r.at[i],
            device_id=dev, device_id_type=MESH,
        )

    def send(src, dst, dev):
        i = count[0]
        count[0] += 1
        copy = make(src, dst, dev, i)
        copy.start()
        started.append(copy)
        return copy

    def ring_start(W):
        return [send(W.at[z], W.at[z], zp)], [send(W.at[z], W.at[z], zm)]

    def ring_step(W, fwd, bwd, half):
        s = len(fwd)
        zf, zb = zi[NZ - s], zi[s]
        fwd[-1].wait_recv()
        if s < 3:
            fwd.append(send(W.at[zf], W.at[zf], zp))
        elif s == 3:
            fwd.append(send(W.at[zf, :, pl.ds(0, half)], W.at[zf, :, pl.ds(0, half)], zp))
        bwd[-1].wait_recv()
        if s < 3:
            bwd.append(send(W.at[zb], W.at[zb], zm))
        elif s == 3:
            bwd.append(send(W.at[zb, :, pl.ds(half, half)], W.at[zb, :, pl.ds(half, half)], zm))

    def exchange(src, Y):
        out = {}
        for e in (1, 3, 2):
            out[e] = send(src.at[yi[e]], Y.at[c, y], {"y": yi[e]})
        Y[c, y] = src[yi[0]]
        return out

    def spread(Y, e, far):
        ref = Y.at[c, yi[e]]
        far["p", e] = send(ref, ref, xp)
        far["m", e] = send(ref, ref, xm)
        far["s", 0, e] = send(ref, ref, sib)

    def onward(Y, e, far):
        left = Y.at[xi[NX - 1] * NK + k, yi[e]]
        right = Y.at[xi[1] * NK + k, yi[e]]
        far["p", e].wait_recv()
        if e in (0, 1):
            far["f", e] = send(left, left, xp)
        far["s", 1, e] = send(left, left, sib)
        far["m", e].wait_recv()
        if e in (2, 3):
            far["f", e] = send(right, right, xm)
        far["s", 2, e] = send(right, right, sib)

    def across(Y, e, far):
        ref = Y.at[xi[2] * NK + k, yi[e]]
        far["f", e].wait_recv()
        far["s", 3, e] = send(ref, ref, sib)

    def gathered(far):
        for i in range(4):
            for e in range(NY):
                far["s", i, e].wait_recv()

    for n in (3, 4):
        loads[n].wait()
    gcol[...] = column(g_row[...])
    x32 = tok[...].astype(f32)
    ssq[c] = jnp.broadcast_to(jnp.sum(x32 * x32, 0, keepdims=True), (8, TOK))
    for i in range(NY):
        here = slice(i * FR, (i + 1) * FR)
        xsrc[i] = (tok[here].astype(f32) * gcol[here]).astype(bf16)
    for n in (0, 1, 2):
        loads[n].wait()
    pl.semaphore_wait(barrier, len(peers))

    a2x = exchange(xsrc, X)
    ring_p = ring_start(Wp)
    fx, fc = {}, {}
    spread(X, 0, fx)
    sq_sent = [send(ssq.at[c], ssq.at[c], dev) for dev in cols]

    for n in (5, 6, 7, 8, 9):
        loads[n].wait()
    own_docs = jnp.concatenate([docs[pl.ds(2 * row, 1), :], docs[pl.ds(2 * row + 1, 1), :]], 1).astype(f32)
    all_docs = docs[...].astype(f32)
    sign = jnp.ones((1, TOK), f32)
    start = jnp.zeros((1, TOK), f32)
    for d in range(NDOC):
        member = (own_docs == d).astype(f32)
        sign = sign - 2.0 * member * labels[d].astype(f32)
        start = start + member * jnp.sum(
            jnp.sum((all_docs < d).astype(f32), 0, keepdims=True), 1, keepdims=True
        )
    lane = lax.broadcasted_iota(jnp.int32, (1, TOK), 1).astype(f32)
    low = jnp.maximum(start - (row * TOK).astype(f32), lane - (WIN - 1.0))
    for i in range(NY):
        csrc[i] = (ups[i * FR : (i + 1) * FR].astype(f32) * sign).astype(bf16)

    for e in (1, 3):
        a2x[4 - e].wait_recv()
        spread(X, e, fx)
    a2c = exchange(csrc, C)
    onward(X, 0, fx)
    a2x[2].wait_recv()
    spread(X, 2, fx)
    ring_step(Wp, *ring_p, 256)
    half = lax.broadcasted_iota(jnp.int32, (HD // 2, TOK), 0).astype(f32)
    place = lax.broadcasted_iota(jnp.int32, (HD // 2, TOK), 1) + row * TOK
    angles = place.astype(f32) * jnp.exp(half * (-2.0 * math.log(10000.0) / HD))
    cs[0] = jnp.cos(angles)
    cs[1] = jnp.sin(angles)
    onward(X, 1, fx)
    onward(X, 3, fx)
    ring_step(Wp, *ring_p, 256)
    onward(X, 2, fx)
    for e in (1, 3, 2):
        a2c[4 - e].wait_recv()
    for e in (0, 1, 3, 2):
        spread(C, e, fc)
    for e in (0, 1, 3):
        across(X, e, fx)
    ring_step(Wp, *ring_p, 256)
    ring_o = ring_start(Wo)
    across(X, 2, fx)
    gathered(fx)
    onward(C, 0, fc)
    ring_step(Wp, *ring_p, 256)

    def partial(u, e):
        total = None
        for i in range(NC):
            if u < 2:
                t = dot(Wp[i, :, u * 256 : u * 256 + 256], X[i, yi[e]], 0, 0)
            else:
                t = dot(Wo[i], C[i, yi[e]], 0, 0)
            total = t if total is None else total + t
        return total

    def reduce_far(u):
        pq[u, 0] = partial(u, 2).astype(bf16)
        return (
            send(pq.at[u, 0, pl.ds(0, 128)], prh.at[u, 0], yp),
            send(pq.at[u, 0, pl.ds(128, 128)], prh.at[u, 1], ym),
        )

    def reduce_near(u, sent):
        t1 = partial(u, 1)
        t3 = partial(u, 3)
        sent[0].wait_recv()
        pq[u, 1, 0:128] = (t1[0:128] + prh[u, 0].astype(f32)).astype(bf16)
        pq[u, 1, 128:256] = t1[128:256].astype(bf16)
        a = send(pq.at[u, 1], pr.at[u, 0], yp)
        sent[1].wait_recv()
        pq[u, 2, 0:128] = t3[0:128].astype(bf16)
        pq[u, 2, 128:256] = (t3[128:256] + prh[u, 1].astype(f32)).astype(bf16)
        b = send(pq.at[u, 2], pr.at[u, 1], ym)
        return a, b

    def reduced(u, own, sent):
        sent[0].wait_recv()
        sent[1].wait_recv()
        return own + pr[u, 0].astype(f32) + pr[u, 1].astype(f32)

    far_k = reduce_far(1)
    far_q = reduce_far(0)
    near_k = reduce_near(1, far_k)
    ring_step(Wo, *ring_o, 128)
    onward(C, 1, fc)
    near_q = reduce_near(0, far_q)
    own_k = partial(1, 0)
    ring_step(Wo, *ring_o, 128)
    onward(C, 3, fc)
    for s in sq_sent:
        s.wait_recv()
    total_sq = ssq[0, 0:1]
    for i in range(1, NC):
        total_sq = total_sq + ssq[i, 0:1]
    scale = lax.rsqrt(total_sq / D + epsilon)
    co, si = cs[0], cs[1]
    qg, kg = column(qg_row[...]), column(kg_row[...])
    kv_proj = reduced(1, own_k, near_k) * scale
    uk, sk = unit(kv_proj[0:128])
    KV[0, 0:128] = rot(uk * kg, co, si).astype(bf16)
    KV[0, 128:256] = kv_proj[128:256].astype(bf16)
    kv_sent = {4: send(KV.at[0], KV.at[4], zp)}
    later = []
    for e in (1, 3, 2):
        i = count[0]
        count[0] += 1
        first = make(KV.at[0], KV.at[e], {"y": yi[e]}, i)
        second = make(KV.at[4], KV.at[e], {"y": yi[e]}, i)
        pl.when(y + e < NY)(first.start)
        later.append((e, second))
        kv_sent[e] = first
        started.append(first)
    onward(C, 2, fc)
    ring_step(Wo, *ring_o, 128)
    across(C, 0, fc)
    own_q = partial(0, 0)
    q_proj = reduced(0, own_q, near_q) * scale
    kv_sent[4].wait_recv()
    for e, second in later:
        pl.when(y + e >= NY)(second.start)
    across(C, 1, fc)
    across(C, 3, fc)
    ring_step(Wo, *ring_o, 128)
    uq0, sq0 = unit(q_proj[0:128])
    uq1, sq1 = unit(q_proj[128:256])
    q = jnp.concatenate([rot(uq0 * qg, co, si), rot(uq1 * qg, co, si)], 1) * query_scale
    q = q.astype(bf16)
    across(C, 2, fc)
    gathered(fc)
    far_o = reduce_far(2)

    low2 = jnp.concatenate([low, low], 1)
    at2 = jnp.concatenate([lane, lane], 1)
    below = lax.broadcasted_iota(jnp.int32, (TOK, 2 * TOK), 0).astype(f32)

    def scores(d, total, attn):
        s = dot(KV[d, 0:128], q, 0, 0)
        ok = below >= low2 + d * TOK
        if d == 0:
            ok = ok & (below <= at2)
        e = jnp.where(ok, jnp.exp(s), 0.0)
        ex[d] = e
        total = total + jnp.sum(e, 0, keepdims=True)
        return total, attn + dot(KV[d, 128:256], e.astype(bf16), 1, 0)

    total, attn = scores(0, jnp.zeros((1, 2 * TOK), f32), jnp.zeros((HD, 2 * TOK), f32))
    near_o = reduce_near(2, far_o)
    own_o = partial(2, 0)
    for d in (4, 1, 3, 2):
        if d < 4:
            kv_sent[d].wait_recv()
        total, attn = scores(d, total, attn)
    inv = 1.0 / total
    attn = attn * inv
    A[y, 0:128] = attn[:, 0:TOK].astype(bf16)
    A[y, 128:256] = attn[:, TOK:].astype(bf16)

    def ag_start(B):
        return [send(B.at[y], B.at[y], yp), send(B.at[y], B.at[y], ym)]

    def ag_step(B, s):
        s[0].wait_recv()
        low_half = B.at[yi[3], pl.ds(0, 128)]
        s.append(send(low_half, low_half, yp))
        s[1].wait_recv()
        high_half = B.at[yi[1], pl.ds(128, 128)]
        s.append(send(high_half, high_half, ym))

    def ag_end(s):
        s[2].wait_recv()
        s[3].wait_recv()

    da = reduced(2, own_o, near_o)
    ag_a = ag_start(A)
    da = jnp.concatenate([da[0:128], da[128:256]], 1).astype(bf16)
    delta = jnp.sum(attn * da.astype(f32), 0, keepdims=True)
    dq = jnp.zeros((HD, 2 * TOK), f32)
    dkv_sent = {}
    for d in (2, 1, 3, 4, 0):
        p = ex[d] * inv
        dp = dot(KV[d, 128:256], da, 0, 0)
        ds = (p * (dp - delta)).astype(bf16)
        dq = dq + dot(KV[d, 0:128], ds, 1, 0)
        dk = dot(q, ds, 1, 1)
        dv = dot(da, p.astype(bf16), 1, 1)
        if d in (1, 2, 3):
            dsb[d - 1, 0:128] = dk.astype(bf16)
            dsb[d - 1, 128:256] = dv.astype(bf16)
            dkv_sent[d] = send(dsb.at[d - 1], drb.at[d - 1], {"y": yi[NY - d]})
        if d == 4:
            dk4, dv4 = dk, dv
    g0 = unit_back(rot(dq[:, 0:TOK], co, -si) * query_scale * qg, uq0, sq0) * scale
    g1 = unit_back(rot(dq[:, TOK:], co, -si) * query_scale * qg, uq1, sq1) * scale
    Gq[y, 0:128] = g0.astype(bf16)
    Gq[y, 128:256] = g1.astype(bf16)
    ag_step(A, ag_a)
    for d in (1, 3, 2):
        dkv_sent[d].wait_recv()
    for d in (1, 2, 3):
        mine = jnp.where(y + d < NY, 1.0, 0.0)
        gk, gv = drb[d - 1, 0:128].astype(f32), drb[d - 1, 128:256].astype(f32)
        dk, dv = dk + gk * mine, dv + gv * mine
        dk4, dv4 = dk4 + gk * (1.0 - mine), dv4 + gv * (1.0 - mine)
    dsb[3, 0:128] = dk4.astype(bf16)
    dsb[3, 128:256] = dv4.astype(bf16)
    dkv_sent[4] = send(dsb.at[3], drb.at[3], zm)
    ag_q = ag_start(Gq)
    ag_end(ag_a)

    stores = [(C, A), (X, Gq), (X, Gk)]

    def part(u, r):
        L, B = stores[u]
        i = zi[r % NZ]
        left = jnp.concatenate([L[i, j] for j in range(NY)], 1)
        right = jnp.concatenate([B[j] for j in range(NY)], 1)
        return dot(left, right, 1, 1)

    zc = {}

    def zs0(u):
        t = part(u, 4).astype(bf16)
        hb[u, 0] = t[:, 0:128]
        hb[u, 1] = t[:, 128:256]
        zc[u, 0, 0] = send(hb.at[u, 0], hr.at[u, 0], zp)
        zc[u, 1, 0] = send(hb.at[u, 1], hr.at[u, 1], zm)

    def zs1(u):
        t = part(u, 3)
        t3 = part(u, -3)
        zc[u, 0, 0].wait_recv()
        sb[u, 0, 0, :, 0:128] = (t[:, 0:128] + hr[u, 0].astype(f32)).astype(bf16)
        sb[u, 0, 0, :, 128:256] = t[:, 128:256].astype(bf16)
        zc[u, 0, 1] = send(sb.at[u, 0, 0], rb.at[u, 0, 0], zp)
        zc[u, 1, 0].wait_recv()
        sb[u, 1, 0, :, 0:128] = t3[:, 0:128].astype(bf16)
        sb[u, 1, 0, :, 128:256] = (t3[:, 128:256] + hr[u, 1].astype(f32)).astype(bf16)
        zc[u, 1, 1] = send(sb.at[u, 1, 0], rb.at[u, 1, 0], zm)

    def zsn(u, n):
        t = [part(u, 4 - n), part(u, n - 4)]
        for w, dev in enumerate((zp, zm)):
            zc[u, w, n - 1].wait_recv()
            sb[u, w, n - 1] = (t[w] + rb[u, w, n - 2].astype(f32)).astype(bf16)
            zc[u, w, n] = send(sb.at[u, w, n - 1], rb.at[u, w, n - 1], dev)

    def zs4(u):
        t = part(u, 0)
        zc[u, 0, 3].wait_recv()
        zc[u, 1, 3].wait_recv()
        return (t + rb[u, 0, 2].astype(f32) + rb[u, 1, 2].astype(f32)).astype(bf16)

    zs0(0)
    dkv_sent[4].wait_recv()
    dk = dk + drb[3, 0:128].astype(f32)
    dv = dv + drb[3, 128:256].astype(f32)
    gk = unit_back(rot(dk, co, -si) * kg, uk, sk) * scale
    gv = dv * scale
    Gk[y, 0:128] = gk.astype(bf16)
    Gk[y, 128:256] = gv.astype(bf16)
    ag_k = ag_start(Gk)
    inner = jnp.sum(
        g0 * q_proj[0:128] + g1 * q_proj[128:256] + gk * kv_proj[0:128] + gv * kv_proj[128:256], 0, keepdims=True
    )
    inn[c] = jnp.broadcast_to(inner, (8, TOK))
    in_sent = [send(inn.at[c], inn.at[c], dev) for dev in cols]
    ag_step(Gq, ag_q)
    zs1(0)
    ag_end(ag_q)
    zs0(1)
    ag_step(Gk, ag_k)
    zsn(0, 2)
    zs1(1)
    ag_end(ag_k)

    def share(i, j):
        j = yi[j]
        g = jnp.concatenate([Gq[j], Gk[j]], 0)
        return dot(Wp[i], g, 1, 0)

    nc = {}

    def to_sibling(r):
        for j in range(NY):
            nb[r, j] = share(xi[r] * NK + ko, j).astype(bf16)
        nc[r] = send(nb.at[r], nr.at[r], sib)

    to_sibling(2)
    to_sibling(1)
    t2 = [share(xi[2] * NK + k, e) for e in range(NY)]
    nc[2].wait_recv()
    xc = {}
    for e in (1, 2, 0, 3):
        mh[e] = (t2[e] + nr[2, e].astype(f32)).astype(bf16)
        xc[e] = send(mh.at[e], mrh.at[e], xp if e < 2 else xm)
    to_sibling(3)
    zs0(2)
    to_sibling(0)
    zsn(0, 3)
    nc[1].wait_recv()
    nc[3].wait_recv()
    mid = {}

    def middle(w, e):
        r = (1, 3)[w]
        t = share(xi[r] * NK + k, e) + nr[r, e].astype(f32)
        if e // 2 == w:
            xc[e].wait_recv()
            t = t + mrh[e].astype(f32)
        mb[w, e] = t.astype(bf16)
        mid[w, e] = send(mb.at[w, e], mr.at[w, e], (xp, xm)[w])

    middle(0, 2)
    middle(1, 1)
    middle(0, 1)
    middle(1, 2)
    zsn(1, 2)
    zs1(2)
    middle(0, 3)
    middle(1, 0)
    middle(0, 0)
    middle(1, 3)
    g_wo[...] = zs4(0)
    zsn(1, 3)
    zsn(2, 2)
    nc[0].wait_recv()
    back = []
    for e in (2, 1, 3, 0):
        t = share(xi[0] * NK + k, e) + nr[0, e].astype(f32)
        mid[0, e].wait_recv()
        mid[1, e].wait_recv()
        t = (t + mr[0, e].astype(f32) + mr[1, e].astype(f32)).astype(bf16)
        if e:
            ds_[e] = t
            back.append(send(ds_.at[e], dr_.at[y], {"y": yi[e]}))
        else:
            dr_[y] = t
        if e == 2:
            zsn(2, 3)
    g_wq[...] = zs4(1)
    for s in in_sent:
        s.wait_recv()
    in_total = inn[0, 0:1]
    for i in range(1, NC):
        in_total = in_total + inn[i, 0:1]
    factor = scale * in_total / D
    last = zs4(2)
    g_wk[...] = last[:, 0:128]
    g_wv[...] = last[:, 128:256]
    for s in back:
        s.wait_recv()
    for j in range(NY):
        here = slice(j * FR, (j + 1) * FR)
        g_in[here] = (dr_[j].astype(f32) * gcol[here] - tok[here].astype(f32) * factor).astype(bf16)
    for s in started:
        s.wait_send()


def hand_over(*refs):
    n = len(refs) // 2
    copies = [pltpu.make_async_copy(refs[i], refs[n + i], refs[-1].at[i]) for i in range(n)]
    for copy in copies:
        copy.start()
    for copy in copies:
        copy.wait()


def per_device(tokens, input_gain, q_gain, k_gain, wq, wk, wv, wo, upstream, doc_ids, doc_labels):
    V = pltpu.VMEM
    piece = (FR, TOK)
    scratch = [
        V((NY * FR, TOK), bf16), V((NY * FR, TOK), bf16), V((1, NY * FR), f32), V((1, HD), f32), V((1, HD), f32),
        V((NZ * NY * TOK // 128, 128), jnp.int32),
        V((NY,) + piece, bf16), V((NY,) + piece, bf16),
        V((NC, NY) + piece, bf16), V((NC, NY) + piece, bf16),
        V((NZ, FR, 512), bf16), V((NZ, FR, 256), bf16),
        V((NC, 8, TOK), f32), V((NC, 8, TOK), f32), V((NY * FR, 1), f32), V((2, HD // 2, TOK), f32),
        V((3, 3, 256, TOK), bf16), V((3, 2, 256, TOK), bf16), V((3, 2, 128, TOK), bf16),
        V((5, 256, TOK), bf16), V((5, TOK, 2 * TOK), f32),
        V((4, 256, TOK), bf16), V((4, 256, TOK), bf16),
        V((NY, 256, TOK), bf16), V((NY, 256, TOK), bf16), V((NY, 256, TOK), bf16),
        V((3, 2, FR, 128), bf16), V((3, 2, FR, 128), bf16),
        V((3, 2, 3, FR, 256), bf16), V((3, 2, 3, FR, 256), bf16),
        V((NX, NY) + piece, bf16), V((NX, NY) + piece, bf16),
        V((NY,) + piece, bf16), V((NY,) + piece, bf16),
        V((2, NY) + piece, bf16), V((2, NY) + piece, bf16),
        V((NY,) + piece, bf16), V((NY,) + piece, bf16),
        pltpu.SemaphoreType.DMA((10,)), pltpu.SemaphoreType.DMA((NSEM,)), pltpu.SemaphoreType.DMA((NSEM,)),
    ]
    vm = pl.BlockSpec(memory_space=pltpu.VMEM)
    hbm = pl.BlockSpec(memory_space=pl.ANY)
    out = [
        jax.ShapeDtypeStruct((NY * FR, TOK), bf16),
        jax.ShapeDtypeStruct((FR, 256), bf16),
        jax.ShapeDtypeStruct((FR, 128), bf16),
        jax.ShapeDtypeStruct((FR, 128), bf16),
        jax.ShapeDtypeStruct((FR, 256), bf16),
    ]
    results = pl.pallas_call(
        kernel,
        out_shape=out,
        in_specs=[hbm] * 10 + [pl.BlockSpec(memory_space=pltpu.SMEM)],
        out_specs=[vm] * 5,
        scratch_shapes=scratch,
        compiler_params=pltpu.CompilerParams(
            collective_id=0, has_side_effects=True, vmem_limit_bytes=60 * 1024 * 1024
        ),
    )(
        tokens.T, upstream.T, input_gain[None, :], q_gain[None, :], k_gain[None, :], wq, wk, wv, wo,
        doc_ids.reshape(-1, 128), doc_labels,
    )
    results = pl.pallas_call(
        hand_over,
        out_shape=out,
        in_specs=[hbm] * 5,
        out_specs=[hbm] * 5,
        scratch_shapes=[pltpu.SemaphoreType.DMA((5,))],
        compiler_params=pltpu.CompilerParams(vmem_limit_bytes=60 * 1024 * 1024),
    )(*results)
    return (results[0].T, *results[1:])


def solution(mesh):
    fine = Mesh(mesh.devices.reshape(NZ, NY, NX, NK), ("z", "y", "x", "k"))
    rc = P(("z", "y"), ("x", "k"))
    return jax.shard_map(
        per_device,
        mesh=fine,
        in_specs=(rc, P(("x", "k")), P(), P(), rc, rc, rc, rc, rc, P(), P()),
        out_specs=(rc,) * 5,
        check_vma=False,
    )
```

time: 132 us -> 136 us (1.030); the launches traced: 130 us -> 136 us
  Pallas kernels: 118 us -> 134 us
  local copies, waits for them, and re-layouts: 10.3 us -> 1.26 us
    pallas_call x1 -> x2, Pallas kernels: 118 us -> 134 us  [the longest x1 114 us: per_device(): pl.pallas_call(kernel, out_shape=out, in_specs=[hbm] * 10 + [pl.BlockSpec...]
    unnamed x24 -> x2, local copies, waits for them, and re-layouts: 4.57 us -> 0.68 us
    pallas_call x1 -> x0, local copies, waits for them, and re-layouts: 1.93 us -> none  [per_device(): pl.pallas_call(kernel, out_shape=out, in_specs=[vm] * 12 + [pl.BlockSpec(...]
    broadcast_in_dim x3 -> x1, local copies, waits for them, and re-layouts: 2.37 us -> 0.58 us  [per_device(): input_gain[None, :]]
    reshape x1 -> x0, local copies, waits for them, and re-layouts: 1.43 us -> none  [per_device(): doc_ids.reshape(NZ * NY, TOK)]
where the time goes in v3:
time: 136 us
  Pallas kernels  134 us (99%)
    pallas_call x1, Pallas kernels, per_device(): pl.pallas_call(kernel, out_shape=out, in_specs=[hbm] * 10 + [pl.BlockSpec...  114 us
    pallas_call x1, Pallas kernels, per_device(): pl.pallas_call(hand_over, out_shape=out, in_specs=[hbm] * 5, out_specs=[h...  19.4 us

profile of v3, /device:TPU:1, one launch (start us, length us, event | category | flops | bytes accessed | tf_op | source)
XLA Modules:
  0.0 135.8 jit_solution(17803630899975180515)
XLA Ops:
  0.6 0.0 copy-start
  0.6 0.7 copy-done
  1.3 0.6 broadcast_in_dim.9.gain
  1.9 114.3 %shard_map.146 = (bf16[672,256]{1,0:T(8,128)(2,1)}, bf16[168,256]{1,0:T(8,128)(2,1)}, bf16[168,128]{1,0:T(8,128)(2,1)}, bf16[168,128]{1,0:T(8,128)(2,1)}, bf16[168,256]{1,0:T(8,128)(2,1)}) custom-call(bf16[672,256]{1,0:T(8,128)(2,1)} %bitcast.6, bf16[672,256]{1,0:T(8,128)(2,1)} %bitcast.7, f32[1,672]{1,0:T(1,128)} %broadcast_in_dim.9.gain, ...), custom_call_target="tpu_custom_call" | custom-call | tf_op jit(solution)/shard_map/pallas_call | solution.py:582
  116.2 19.4 %shard_map.147 = (bf16[672,256]{1,0:T(8,128)(2,1)}, bf16[168,256]{1,0:T(8,128)(2,1)}, bf16[168,128]{1,0:T(8,128)(2,1)}, bf16[168,128]{1,0:T(8,128)(2,1)}, bf16[168,256]{1,0:T(8,128)(2,1)}) custom-call(bf16[672,256]{1,0:T(8,128)(2,1)} %get-tuple-element.15.refs_0_, bf16[168,256]{1,0:T(8,128)(2,1)} %get-tuple-element.16.refs_1_, ...), custom_call_target="tpu_custom_call" | custom-call | tf_op jit(solution)/shard_map/pallas_call | solution.py:595
Async XLA Ops:
  0.6 0.7 copy-start

commit v4 on v3

--- a/solution.py
+++ b/solution.py
@@ -541,11 +541,8 @@
 
 def hand_over(*refs):
     n = len(refs) // 2
-    copies = [pltpu.make_async_copy(refs[i], refs[n + i], refs[-1].at[i]) for i in range(n)]
-    for copy in copies:
-        copy.start()
-    for copy in copies:
-        copy.wait()
+    for i in range(n):
+        refs[n + i][...] = refs[i][...]
 
 
 def per_device(tokens, input_gain, q_gain, k_gain, wq, wk, wv, wo, upstream, doc_ids, doc_labels):
@@ -595,10 +592,8 @@
     results = pl.pallas_call(
         hand_over,
         out_shape=out,
-        in_specs=[hbm] * 5,
-        out_specs=[hbm] * 5,
-        scratch_shapes=[pltpu.SemaphoreType.DMA((5,))],
-        compiler_params=pltpu.CompilerParams(vmem_limit_bytes=60 * 1024 * 1024),
+        in_specs=[vm] * 5,
+        out_specs=[vm] * 5,
     )(*results)
     return (results[0].T, *results[1:])
 

time: 136 us -> 118 us (0.87)
  Pallas kernels: 134 us -> 116 us
    pallas_call x1, Pallas kernels: 19.4 us -> 1.9 us  [per_device(): pl.pallas_call(hand_over, out_shape=out, in_specs=[vm] * 5, out_specs=[vm...]
where the time goes in v4:
time: 118 us
  Pallas kernels  116 us (98%)
  local copies, waits for them, and re-layouts  1.26 us (1%)
    pallas_call x1, Pallas kernels, per_device(): pl.pallas_call(kernel, out_shape=out, in_specs=[hbm] * 10 + [pl.BlockSpec...  114 us

profile of v4, /device:TPU:1, one launch (start us, length us, event | category | flops | bytes accessed | tf_op | source)
XLA Modules:
  0.0 118.1 jit_solution(4524669155753800031)
XLA Ops:
  0.6 0.0 copy-start
  0.6 0.7 copy-done
  1.3 0.6 broadcast_in_dim.9.gain
  1.9 114.3 %shard_map.146 = (bf16[672,256]{1,0:T(8,128)(2,1)}, bf16[168,256]{1,0:T(8,128)(2,1)}, bf16[168,128]{1,0:T(8,128)(2,1)}, bf16[168,128]{1,0:T(8,128)(2,1)}, bf16[168,256]{1,0:T(8,128)(2,1)}) custom-call(bf16[672,256]{1,0:T(8,128)(2,1)} %bitcast.6, bf16[672,256]{1,0:T(8,128)(2,1)} %bitcast.7, f32[1,672]{1,0:T(1,128)} %broadcast_in_dim.9.gain, ...), custom_call_target="tpu_custom_call" | custom-call | tf_op jit(solution)/shard_map/pallas_call | solution.py:579
  116.2 1.9 %shard_map.147 = (bf16[672,256]{1,0:T(8,128)(2,1)}, bf16[168,256]{1,0:T(8,128)(2,1)}, bf16[168,128]{1,0:T(8,128)(2,1)}, bf16[168,128]{1,0:T(8,128)(2,1)}, bf16[168,256]{1,0:T(8,128)(2,1)}) custom-call(bf16[672,256]{1,0:T(8,128)(2,1)} %get-tuple-element.15.refs_0_, bf16[168,256]{1,0:T(8,128)(2,1)} %get-tuple-element.16.refs_1_, ...), custom_call_target="tpu_custom_call" | custom-call | tf_op jit(solution)/shard_map/pallas_call | solution.py:592
Async XLA Ops:
  0.6 0.7 copy-start

commit v5 on v4

--- a/solution.py
+++ b/solution.py
@@ -109,6 +109,11 @@
         started.append(copy)
         return copy
 
+    def settle(n):
+        for s in started[:n]:
+            s.wait_send()
+        del started[:n]
+
     def ring_start(W):
         return [send(W.at[z], W.at[z], zp)], [send(W.at[z], W.at[z], zm)]
 
@@ -163,7 +168,7 @@
 
     for n in (3, 4):
         loads[n].wait()
-    gcol[...] = column(g_row[...])
+    gcol[...] = column(g_row[...].reshape(1, NY * FR))
     x32 = tok[...].astype(f32)
     ssq[c] = jnp.broadcast_to(jnp.sum(x32 * x32, 0, keepdims=True), (8, TOK))
     for i in range(NY):
@@ -204,11 +209,6 @@
     a2x[2].wait_recv()
     spread(X, 2, fx)
     ring_step(Wp, *ring_p, 256)
-    half = lax.broadcasted_iota(jnp.int32, (HD // 2, TOK), 0).astype(f32)
-    place = lax.broadcasted_iota(jnp.int32, (HD // 2, TOK), 1) + row * TOK
-    angles = place.astype(f32) * jnp.exp(half * (-2.0 * math.log(10000.0) / HD))
-    cs[0] = jnp.cos(angles)
-    cs[1] = jnp.sin(angles)
     onward(X, 1, fx)
     onward(X, 3, fx)
     ring_step(Wp, *ring_p, 256)
@@ -261,12 +261,17 @@
         sent[1].wait_recv()
         return own + pr[u, 0].astype(f32) + pr[u, 1].astype(f32)
 
+    old = len(started)
     far_k = reduce_far(1)
     far_q = reduce_far(0)
+    half = lax.broadcasted_iota(jnp.int32, (HD // 2, TOK), 0).astype(f32)
+    place = lax.broadcasted_iota(jnp.int32, (HD // 2, TOK), 1) + row * TOK
+    angles = place.astype(f32) * jnp.exp(half * (-2.0 * math.log(10000.0) / HD))
+    cs[0] = jnp.cos(angles)
+    cs[1] = jnp.sin(angles)
     near_k = reduce_near(1, far_k)
     ring_step(Wo, *ring_o, 128)
     onward(C, 1, fc)
-    near_q = reduce_near(0, far_q)
     own_k = partial(1, 0)
     ring_step(Wo, *ring_o, 128)
     onward(C, 3, fc)
@@ -282,25 +287,32 @@
     uk, sk = unit(kv_proj[0:128])
     KV[0, 0:128] = rot(uk * kg, co, si).astype(bf16)
     KV[0, 128:256] = kv_proj[128:256].astype(bf16)
-    kv_sent = {4: send(KV.at[0], KV.at[4], zp)}
-    later = []
-    for e in (1, 3, 2):
-        i = count[0]
-        count[0] += 1
-        first = make(KV.at[0], KV.at[e], {"y": yi[e]}, i)
-        second = make(KV.at[4], KV.at[e], {"y": yi[e]}, i)
-        pl.when(y + e < NY)(first.start)
-        later.append((e, second))
-        kv_sent[e] = first
-        started.append(first)
+    kv_sent, later = {}, []
+    halves = (pl.ds(0, 128), pl.ds(128, 128))
+    for h in (0, 1):
+        kv_sent[4, h] = send(KV.at[0, halves[h]], KV.at[4, halves[h]], zp)
+    for h in (0, 1):
+        for e in (1, 3, 2):
+            i = count[0]
+            count[0] += 1
+            first = make(KV.at[0, halves[h]], KV.at[e, halves[h]], {"y": yi[e]}, i)
+            second = make(KV.at[4, halves[h]], KV.at[e, halves[h]], {"y": yi[e]}, i)
+            pl.when(y + e < NY)(first.start)
+            later.append((e, h, second))
+            kv_sent[e, h] = first
+            started.append(first)
+    near_q = reduce_near(0, far_q)
+    settle(old)
     onward(C, 2, fc)
     ring_step(Wo, *ring_o, 128)
     across(C, 0, fc)
     own_q = partial(0, 0)
+    for h in (0, 1):
+        kv_sent[4, h].wait_recv()
+        for e, g, second in later:
+            if g == h:
+                pl.when(y + e >= NY)(second.start)
     q_proj = reduced(0, own_q, near_q) * scale
-    kv_sent[4].wait_recv()
-    for e, second in later:
-        pl.when(y + e >= NY)(second.start)
     across(C, 1, fc)
     across(C, 3, fc)
     ring_step(Wo, *ring_o, 128)
@@ -312,6 +324,7 @@
     gathered(fc)
     far_o = reduce_far(2)
 
+    old = len(started)
     low2 = jnp.concatenate([low, low], 1)
     at2 = jnp.concatenate([lane, lane], 1)
     below = lax.broadcasted_iota(jnp.int32, (TOK, 2 * TOK), 0).astype(f32)
@@ -331,7 +344,8 @@
     own_o = partial(2, 0)
     for d in (4, 1, 3, 2):
         if d < 4:
-            kv_sent[d].wait_recv()
+            kv_sent[d, 0].wait_recv()
+            kv_sent[d, 1].wait_recv()
         total, attn = scores(d, total, attn)
     inv = 1.0 / total
     attn = attn * inv
@@ -369,24 +383,29 @@
         if d in (1, 2, 3):
             dsb[d - 1, 0:128] = dk.astype(bf16)
             dsb[d - 1, 128:256] = dv.astype(bf16)
-            dkv_sent[d] = send(dsb.at[d - 1], drb.at[d - 1], {"y": yi[NY - d]})
+            dkv_sent[d, 0] = send(dsb.at[d - 1, halves[0]], drb.at[d - 1, halves[0]], {"y": yi[NY - d]})
         if d == 4:
             dk4, dv4 = dk, dv
+    for d in (2, 1, 3):
+        dkv_sent[d, 1] = send(dsb.at[d - 1, halves[1]], drb.at[d - 1, halves[1]], {"y": yi[NY - d]})
     g0 = unit_back(rot(dq[:, 0:TOK], co, -si) * query_scale * qg, uq0, sq0) * scale
     g1 = unit_back(rot(dq[:, TOK:], co, -si) * query_scale * qg, uq1, sq1) * scale
     Gq[y, 0:128] = g0.astype(bf16)
     Gq[y, 128:256] = g1.astype(bf16)
     ag_step(A, ag_a)
-    for d in (1, 3, 2):
-        dkv_sent[d].wait_recv()
-    for d in (1, 2, 3):
-        mine = jnp.where(y + d < NY, 1.0, 0.0)
-        gk, gv = drb[d - 1, 0:128].astype(f32), drb[d - 1, 128:256].astype(f32)
-        dk, dv = dk + gk * mine, dv + gv * mine
-        dk4, dv4 = dk4 + gk * (1.0 - mine), dv4 + gv * (1.0 - mine)
-    dsb[3, 0:128] = dk4.astype(bf16)
-    dsb[3, 128:256] = dv4.astype(bf16)
-    dkv_sent[4] = send(dsb.at[3], drb.at[3], zm)
+    settle(old)
+    old = len(started)
+    sums = [[dk, dk4], [dv, dv4]]
+    for h in (0, 1):
+        for d in (1, 3, 2):
+            dkv_sent[d, h].wait_recv()
+        for d in (1, 2, 3):
+            mine = jnp.where(y + d < NY, 1.0, 0.0)
+            got = drb[d - 1, h * 128 : h * 128 + 128].astype(f32)
+            sums[h][0] = sums[h][0] + got * mine
+            sums[h][1] = sums[h][1] + got * (1.0 - mine)
+        dsb[3, h * 128 : h * 128 + 128] = sums[h][1].astype(bf16)
+        dkv_sent[4, h] = send(dsb.at[3, halves[h]], drb.at[3, halves[h]], zm)
     ag_q = ag_start(Gq)
     ag_end(ag_a)
 
@@ -434,14 +453,27 @@
         return (t + rb[u, 0, 2].astype(f32) + rb[u, 1, 2].astype(f32)).astype(bf16)
 
     zs0(0)
-    dkv_sent[4].wait_recv()
-    dk = dk + drb[3, 0:128].astype(f32)
-    dv = dv + drb[3, 128:256].astype(f32)
+    def half_start(h):
+        ref = Gk.at[y, halves[h]]
+        return [send(ref, ref, yp), send(ref, ref, ym)]
+
+    def half_step(h, s):
+        s[0].wait_recv()
+        ref = Gk.at[yi[3], pl.ds(h * 128, 64)]
+        s.append(send(ref, ref, yp))
+        s[1].wait_recv()
+        ref = Gk.at[yi[1], pl.ds(h * 128 + 64, 64)]
+        s.append(send(ref, ref, ym))
+
+    dkv_sent[4, 0].wait_recv()
+    dk = sums[0][0] + drb[3, 0:128].astype(f32)
     gk = unit_back(rot(dk, co, -si) * kg, uk, sk) * scale
-    gv = dv * scale
     Gk[y, 0:128] = gk.astype(bf16)
+    ag_k = half_start(0)
+    dkv_sent[4, 1].wait_recv()
+    gv = (sums[1][0] + drb[3, 128:256].astype(f32)) * scale
     Gk[y, 128:256] = gv.astype(bf16)
-    ag_k = ag_start(Gk)
+    ag_v = half_start(1)
     inner = jnp.sum(
         g0 * q_proj[0:128] + g1 * q_proj[128:256] + gk * kv_proj[0:128] + gv * kv_proj[128:256], 0, keepdims=True
     )
@@ -451,10 +483,12 @@
     zs1(0)
     ag_end(ag_q)
     zs0(1)
-    ag_step(Gk, ag_k)
+    half_step(0, ag_k)
+    half_step(1, ag_v)
     zsn(0, 2)
     zs1(1)
     ag_end(ag_k)
+    ag_end(ag_v)
 
     def share(i, j):
         j = yi[j]
@@ -469,6 +503,7 @@
         nc[r] = send(nb.at[r], nr.at[r], sib)
 
     to_sibling(2)
+    zs0(2)
     to_sibling(1)
     t2 = [share(xi[2] * NK + k, e) for e in range(NY)]
     nc[2].wait_recv()
@@ -477,11 +512,12 @@
         mh[e] = (t2[e] + nr[2, e].astype(f32)).astype(bf16)
         xc[e] = send(mh.at[e], mrh.at[e], xp if e < 2 else xm)
     to_sibling(3)
-    zs0(2)
     to_sibling(0)
     zsn(0, 3)
     nc[1].wait_recv()
     nc[3].wait_recv()
+    settle(old)
+    old = len(started)
     mid = {}
 
     def middle(w, e):
@@ -500,13 +536,14 @@
     zsn(1, 2)
     zs1(2)
     middle(0, 3)
+    middle(1, 3)
+    middle(0, 0)
     middle(1, 0)
-    middle(0, 0)
-    middle(1, 3)
+    zsn(1, 3)
     g_wo[...] = zs4(0)
-    zsn(1, 3)
     zsn(2, 2)
     nc[0].wait_recv()
+    settle(old)
     back = []
     for e in (2, 1, 3, 0):
         t = share(xi[0] * NK + k, e) + nr[0, e].astype(f32)
@@ -549,7 +586,7 @@
     V = pltpu.VMEM
     piece = (FR, TOK)
     scratch = [
-        V((NY * FR, TOK), bf16), V((NY * FR, TOK), bf16), V((1, NY * FR), f32), V((1, HD), f32), V((1, HD), f32),
+        V((NY * FR, TOK), bf16), V((NY * FR, TOK), bf16), V((NY * FR,), f32), V((1, HD), f32), V((1, HD), f32),
         V((NZ * NY * TOK // 128, 128), jnp.int32),
         V((NY,) + piece, bf16), V((NY,) + piece, bf16),
         V((NC, NY) + piece, bf16), V((NC, NY) + piece, bf16),
@@ -586,7 +623,7 @@
             collective_id=0, has_side_effects=True, vmem_limit_bytes=60 * 1024 * 1024
         ),
     )(
-        tokens.T, upstream.T, input_gain[None, :], q_gain[None, :], k_gain[None, :], wq, wk, wv, wo,
+        tokens.T, upstream.T, input_gain, q_gain[None, :], k_gain[None, :], wq, wk, wv, wo,
         doc_ids.reshape(-1, 128), doc_labels,
     )
     results = pl.pallas_call(

time: 118 us -> 115 us (0.975)
  local copies, waits for them, and re-layouts: 1.26 us -> 0 us
    pallas_call x1, Pallas kernels: 114 us -> 113 us  [per_device(): pl.pallas_call(kernel, out_shape=out, in_specs=[hbm] * 10 + [pl.BlockSpec...]
where the time goes in v5:
time: 115 us
  Pallas kernels  115 us (100%)
    pallas_call x1, Pallas kernels, per_device(): pl.pallas_call(kernel, out_shape=out, in_specs=[hbm] * 10 + [pl.BlockSpec...  113 us

profile of v5, /device:TPU:1, one launch (start us, length us, event | category | flops | bytes accessed | tf_op | source)
XLA Modules:
  0.0 115.1 jit_solution(5583795859392612612)
XLA Ops:
  0.6 112.6 %shard_map.146 = (bf16[672,256]{1,0:T(8,128)(2,1)}, bf16[168,256]{1,0:T(8,128)(2,1)}, bf16[168,128]{1,0:T(8,128)(2,1)}, bf16[168,128]{1,0:T(8,128)(2,1)}, bf16[168,256]{1,0:T(8,128)(2,1)}) custom-call(bf16[672,256]{1,0:T(8,128)(2,1)} %bitcast.6, bf16[672,256]{1,0:T(8,128)(2,1)} %bitcast.7, f32[672]{0:T(1024)} %gain.1, f32[1,128]{1,0:T(1,128)} %bitcast.9, ...), custom_call_target="tpu_custom_call" | custom-call | tf_op jit(solution)/shard_map/pallas_call | solution.py:616
  113.2 1.9 %shard_map.147 = (bf16[672,256]{1,0:T(8,128)(2,1)}, bf16[168,256]{1,0:T(8,128)(2,1)}, bf16[168,128]{1,0:T(8,128)(2,1)}, bf16[168,128]{1,0:T(8,128)(2,1)}, bf16[168,256]{1,0:T(8,128)(2,1)}) custom-call(bf16[672,256]{1,0:T(8,128)(2,1)} %get-tuple-element.15.refs_0_, bf16[168,256]{1,0:T(8,128)(2,1)} %get-tuple-element.16.refs_1_, ...), custom_call_target="tpu_custom_call" | custom-call | tf_op jit(solution)/shard_map/pallas_call | solution.py:629

commit v6 on v5

--- a/solution.py
+++ b/solution.py
@@ -504,13 +504,13 @@
 
     to_sibling(2)
     zs0(2)
-    to_sibling(1)
     t2 = [share(xi[2] * NK + k, e) for e in range(NY)]
     nc[2].wait_recv()
     xc = {}
     for e in (1, 2, 0, 3):
         mh[e] = (t2[e] + nr[2, e].astype(f32)).astype(bf16)
         xc[e] = send(mh.at[e], mrh.at[e], xp if e < 2 else xm)
+    to_sibling(1)
     to_sibling(3)
     to_sibling(0)
     zsn(0, 3)

time: 115 us -> 116 us (level)
  no operation moved by 1% of the time
where the time goes in v6:
time: 116 us
  Pallas kernels  115 us (99%)
    pallas_call x1, Pallas kernels, per_device(): pl.pallas_call(kernel, out_shape=out, in_specs=[hbm] * 10 + [pl.BlockSpec...  113 us

profile of v6, /device:TPU:1, one launch (start us, length us, event | category | flops | bytes accessed | tf_op | source)
XLA Modules:
  0.0 115.7 jit_solution(14304140515732406280)
XLA Ops:
  0.6 113.2 %shard_map.146 = (bf16[672,256]{1,0:T(8,128)(2,1)}, bf16[168,256]{1,0:T(8,128)(2,1)}, bf16[168,128]{1,0:T(8,128)(2,1)}, bf16[168,128]{1,0:T(8,128)(2,1)}, bf16[168,256]{1,0:T(8,128)(2,1)}) custom-call(bf16[672,256]{1,0:T(8,128)(2,1)} %bitcast.6, bf16[672,256]{1,0:T(8,128)(2,1)} %bitcast.7, f32[672]{0:T(1024)} %gain.1, f32[1,128]{1,0:T(1,128)} %bitcast.9, ...), custom_call_target="tpu_custom_call" | custom-call | tf_op jit(solution)/shard_map/pallas_call | solution.py:616
  113.8 1.9 %shard_map.147 = (bf16[672,256]{1,0:T(8,128)(2,1)}, bf16[168,256]{1,0:T(8,128)(2,1)}, bf16[168,128]{1,0:T(8,128)(2,1)}, bf16[168,128]{1,0:T(8,128)(2,1)}, bf16[168,256]{1,0:T(8,128)(2,1)}) custom-call(bf16[672,256]{1,0:T(8,128)(2,1)} %get-tuple-element.15.refs_0_, bf16[168,256]{1,0:T(8,128)(2,1)} %get-tuple-element.16.refs_1_, ...), custom_call_target="tpu_custom_call" | custom-call | tf_op jit(solution)/shard_map/pallas_call | solution.py:629
